TPU v7x, 256 devices: a whole 4x4x8 slice. The times are simulated.
256 devices in a mesh: lon: 64 (over x_hi, y, z), lat: 4 (over x_lo, core).
Axes of the slice: x: 4 (x_hi: 2, x_lo: 2; x = x_hi * 2 + x_lo), y: 4, z: 8, core: 2. Of those that a mesh axis runs over, the one named last changes fastest.
Arguments:
- queries: bfloat16 [4, 64, 128, 1536], P(None, 'lat', 'lon'), may hold values from -100 to 100
- token_keys: bfloat16 [4, 64, 128, 1536], P(None, 'lat', 'lon'), may hold values from -6 to 6
- token_values: bfloat16 [4, 64, 128, 1536], P(None, 'lat', 'lon'), may hold values from -6 to 6
- memory_bank: bfloat16 [2, 8, 64, 128, 1536], P(None, None, 'lat', 'lon'), may hold values from -6 to 6
- memory_ids: int32 [4, 64, 8], P('lat', 'lon'), may hold values from 0 to 511, as said below
- memory_count: int32 [4, 64], P('lat', 'lon'), may hold values from 7 to 8
Outputs:
- attended: bfloat16 [4, 64, 128, 1536], P(None, 'lat', 'lon')
Inputs may be any that keep to these rules, and one draw needn't show every extreme that they name: `memory_ids`: entry v of tile (a, b) names slot v mod 8 of the tile (a, v // 8) of the same band, whose longitude tile lies within 2 tiles of b around the closed loop. Within one list no block appears twice and at most 4 entries name one owner tile; the first 4 entries all name one owner tile.
All inputs are finite; a program needn't handle non-finite values.
Results may differ from a plain program's by a relative error of at most 0.003.
Values may be sent and summed in bfloat16 or wider, within the bound.
No kernel may reach another device: no remote copies, remote signals or barrier semaphores. Data moves between devices by JAX's collectives and lax.ppermute only.
A program may use at most 64 MiB of HBM per device.

v0:
```python
import math

import jax
import jax.numpy as jnp
from jax import lax
from jax.sharding import PartitionSpec as P

HEADS = 12
HEAD_DIM = 128
REACH = 2


MASKED = -1e30


def from_behind(value, axis, steps):
    count = lax.axis_size(axis)
    first, last = (max(0, -steps), min(count, count - steps))
    return lax.ppermute(value, axis, [(source, source + steps) for source in range(first, last)])


def extended(block, sides, width):
    for axis, dim in sides:
        count = lax.axis_size(axis)
        forward = [(i, i + 1) for i in range(count - 1)]
        forward.append((count - 1, 0))
        backward = [(target, source) for source, target in forward]
        low = lax.ppermute(
            lax.slice_in_dim(block, block.shape[dim] - width, None, axis=dim), axis, forward
        )
        high = lax.ppermute(lax.slice_in_dim(block, 0, width, axis=dim), axis, backward)
        block = jnp.concatenate([low, block, high], axis=dim)
    return block


def passed_along(block, axis, distance):
    devices = range(lax.axis_size(axis))
    route = [((i - distance) % len(devices), i) for i in devices]
    return lax.ppermute(block, axis, route)


def attend(query_rows, key_rows, value_rows, valid):
    count_q = query_rows.shape[0]
    group_size = math.gcd(HEADS, 4)
    blocks = HEADS // group_size
    scaling = HEAD_DIM ** (-0.5)

    def split_heads(matrix):
        return jnp.moveaxis(matrix.reshape(matrix.shape[0], blocks, group_size, HEAD_DIM), 1, 0)

    def one_block(operands):
        query_part, key_part, value_part = operands
        scores = (
            jnp.einsum("qgd,kgd->gqk", query_part, key_part, preferred_element_type=jnp.float32)
            * scaling
        )
        scores = jnp.where(valid[None, None, :], scores, MASKED)
        largest = jnp.max(scores, axis=2, keepdims=True)
        weights = jnp.exp(scores - largest)
        totals = jnp.sum(weights, axis=2)
        mixture = jnp.einsum(
            "gqk,kgd->qgd",
            weights.astype(jnp.bfloat16),
            value_part,
            preferred_element_type=jnp.float32,
        )
        return mixture / jnp.transpose(totals)[:, :, None]

    results = lax.map(
        one_block, (split_heads(query_rows), split_heads(key_rows), split_heads(value_rows))
    )
    return jnp.moveaxis(results, 0, 1).reshape(count_q, HEADS * HEAD_DIM)


def local(queries, token_keys, token_values, memory_bank, memory_ids, memory_count):
    frames, band_rows, tile_cols, feature_width = queries.shape
    row_count = frames * band_rows * tile_cols
    mem_slots = memory_bank.shape[1]
    stacked = jnp.stack([token_keys, token_values])
    band_index = lax.axis_index("lat")
    band_count = lax.axis_size("lat")
    rim_list = []
    for shift_by in (1, -1):
        rim_list.append(from_behind(stacked, "lat", shift_by))
    tall_region = jnp.concatenate([rim_list[0], stacked, rim_list[1]], axis=2)
    region = extended(tall_region, (("lon", 3),), tile_cols)
    row_valid = jnp.concatenate(
        [
            jnp.full((band_rows,), band_index > 0),
            jnp.ones((band_rows,), bool),
            jnp.full((band_rows,), band_index < band_count - 1),
        ]
    )
    near_valid = jnp.broadcast_to(
        row_valid[None, :, None], (frames, 3 * band_rows, 3 * tile_cols)
    ).reshape(-1)
    flat_queries = queries.reshape(row_count, feature_width)
    near_out = attend(
        flat_queries,
        region[0].reshape(-1, feature_width),
        region[1].reshape(-1, feature_width),
        near_valid,
    )
    sector = lax.axis_index("lon")
    sector_count = lax.axis_size("lon")
    block_ids = memory_ids.reshape(-1)
    live_count = memory_count.reshape(())
    owner_col = block_ids // mem_slots
    slot_index = block_ids % mem_slots
    offset = (owner_col - sector + REACH) % sector_count - REACH
    live_entry = jnp.arange(block_ids.shape[0]) < live_count
    block_tokens = band_rows * tile_cols
    shelves = []
    for shift_by in range(-REACH, REACH + 1):
        if shift_by == 0:
            shelves.append(memory_bank)
        else:
            shelves.append(passed_along(memory_bank, "lon", -shift_by))
    library = jnp.stack(shelves)
    picked = library[offset + REACH, :, slot_index]
    memory_keys = picked[:, 0].reshape(-1, feature_width)
    memory_values = picked[:, 1].reshape(-1, feature_width)
    far_valid = jnp.repeat(live_entry, block_tokens)
    far_out = attend(flat_queries, memory_keys, memory_values, far_valid)
    return (
        (near_out + far_out)
        .astype(jnp.bfloat16)
        .reshape(frames, band_rows, tile_cols, feature_width)
    )


def solution(mesh):
    placed = (
        P(None, "lat", "lon", None),
        P(None, "lat", "lon", None),
        P(None, "lat", "lon", None),
        P(None, None, "lat", "lon", None),
        P("lat", "lon", None),
        P("lat", "lon"),
    )
    return jax.shard_map(
        local, mesh=mesh, in_specs=placed, out_specs=P(None, "lat", "lon", None), check_vma=False
    )
```

profile of v0, /device:TPU:1, one launch (start us, length us, event | category | flops | bytes accessed | tf_op | source)
XLA Modules:
  0.0 237.2 jit_solution(15498933328263698002)
XLA Ops:
  0.0 3.3 %pad_maximum_fusion.2 = bf16[2,4,16,2,1536]{4,3,2,1,0:T(2,128)(2,1)} fusion(bf16[1,4,16,2,1536]{4,3,2,1,0:T(2,128)(2,1)} %bitcast.126, bf16[1,4,16,2,1536]{4,3,2,1,0:T(2,128)(2,1)} %bitcast.129), kind=kLoop, calls=%fused_computation.45 | loop fusion | flops 393216 | bytes 1572864 | tf_op jit(solution)/shard_map/stack | solution.py:79
  3.3 4.5 %collective-permute-start = (bf16[2,4,16,2,1536]{4,3,2,1,0:T(2,128)(2,1)}, bf16[2,4,16,2,1536]{4,3,2,1,0:T(2,128)(2,1)S(1)}, u32[]{:S(2)}, u32[]{:S(2)}) collective-permute-start(bf16[2,4,16,2,1536]{4,3,2,1,0:T(2,128)(2,1)} %pad_maximum_fusion.2), channel_id=1, source_target_pairs={{0,1},{1,2},{2,3},{4,5},{5,6},{6,7},{8,9},{9,10},{10,11},{12,13},{... | collective-permute-start | bytes 2359304 | tf_op jit(solution)/shard_map/ppermute | solution.py:19
  9.8 3.0 %collective-permute-start.4 = (bf16[2,8,16,2,1536]{4,3,2,1,0:T(2,128)(2,1)}, bf16[2,8,16,2,1536]{4,3,2,1,0:T(2,128)(2,1)}, u32[]{:S(2)}, u32[]{:S(2)}) collective-permute-start(bf16[2,8,16,2,1536]{4,3,2,1,0:T(2,128)(2,1)} %param.13), channel_id=1, source_target_pairs={{248,0},{252,4},{0,8},{4,12},{8,16},{12,20},{16,24},{20,28},{24,32... | collective-permute-start | bytes 4718600 | tf_op jit(solution)/shard_map/ppermute | solution.py:39
  14.4 5.7 %collective-permute-start.6 = (bf16[2,8,16,2,1536]{4,3,2,1,0:T(2,128)(2,1)}, bf16[2,8,16,2,1536]{4,3,2,1,0:T(2,128)(2,1)}, u32[]{:S(2)}, u32[]{:S(2)}) collective-permute-start(bf16[2,8,16,2,1536]{4,3,2,1,0:T(2,128)(2,1)} %param.13), channel_id=1, source_target_pairs={{4,0},{8,4},{12,8},{16,12},{20,16},{24,20},{28,24},{32,28},{36,32}... | collective-permute-start | bytes 4718600 | tf_op jit(solution)/shard_map/ppermute | solution.py:39
  22.3 5.3 %collective-permute-start.7 = (bf16[2,8,16,2,1536]{4,3,2,1,0:T(2,128)(2,1)}, bf16[2,8,16,2,1536]{4,3,2,1,0:T(2,128)(2,1)S(1)}, u32[]{:S(2)}, u32[]{:S(2)}) collective-permute-start(bf16[2,8,16,2,1536]{4,3,2,1,0:T(2,128)(2,1)} %param.13), channel_id=1, source_target_pairs={{8,0},{12,4},{16,8},{20,12},{24,16},{28,20},{32,24},{36,28},{40,32... | collective-permute-start | bytes 4718600 | tf_op jit(solution)/shard_map/ppermute | solution.py:39
  27.7 4.4 %pad_maximum_fusion.1 = bf16[2,4,48,2,1536]{4,3,2,1,0:T(2,128)(2,1)} fusion(bf16[2,4,16,2,1536]{4,3,2,1,0:T(2,128)(2,1)S(1)} %collective-permute-done.1, bf16[1,4,16,2,1536]{4,3,2,1,0:T(2,128)(2,1)S(1)} %bitcast.127, bf16[1,4,16,2,1536]{4,3,2,1,0:T(2,128)(2,1)S(1)} %bitcast.131, bf16[2,4,16,2,1536]{4,3,2,1,0:T(2,128)(2,1)S(1)} %collective-permute-done), kind=kLoop, calls=%fused_computation.39 | loop fusion | flops 3538944 | bytes 4718592 | tf_op jit(solution)/shard_map/concatenate | solution.py:85
  32.9 56.0 %collective-permute-done.4 = bf16[2,8,16,2,1536]{4,3,2,1,0:T(2,128)(2,1)} collective-permute-done((bf16[2,8,16,2,1536]{4,3,2,1,0:T(2,128)(2,1)}, bf16[2,8,16,2,1536]{4,3,2,1,0:T(2,128)(2,1)}, u32[]{:S(2)}, u32[]{:S(2)}) %collective-permute-start.4) | collective-permute-done | bytes 1572896 | tf_op jit(solution)/shard_map/ppermute | solution.py:39
  90.2 3.7 %bitcast_dynamic-update-slice_fusion.4 = bf16[5,2,8,16,2,1536]{5,4,3,2,1,0:T(2,128)(2,1)} fusion(bf16[2,8,16,2,1536]{4,3,2,1,0:T(2,128)(2,1)} %collective-permute-done.4), kind=kLoop, calls=%fused_computation.44 | loop fusion | bytes 3145728
  94.0 27.9 %collective-permute-done.5 = bf16[2,8,16,2,1536]{4,3,2,1,0:T(2,128)(2,1)} collective-permute-done((bf16[2,8,16,2,1536]{4,3,2,1,0:T(2,128)(2,1)}, bf16[2,8,16,2,1536]{4,3,2,1,0:T(2,128)(2,1)}, u32[]{:S(2)}, u32[]{:S(2)}) %collective-permute-start.5) | collective-permute-done | bytes 1572896 | tf_op jit(solution)/shard_map/ppermute | solution.py:39
  121.9 3.7 %bitcast_dynamic-update-slice_fusion.3 = bf16[5,2,8,16,2,1536]{5,4,3,2,1,0:T(2,128)(2,1)} fusion(bf16[5,2,8,16,2,1536]{5,4,3,2,1,0:T(2,128)(2,1)} %bitcast_dynamic-update-slice_fusion.4, bf16[2,8,16,2,1536]{4,3,2,1,0:T(2,128)(2,1)} %collective-permute-done.5), kind=kLoop, calls=%fused_computation.43 | loop fusion | bytes 3145728
  127.9 3.7 %bitcast_dynamic-update-slice_fusion.1 = bf16[5,2,8,16,2,1536]{5,4,3,2,1,0:T(2,128)(2,1)} fusion(bf16[5,2,8,16,2,1536]{5,4,3,2,1,0:T(2,128)(2,1)} %bitcast_dynamic-update-slice_fusion.2, bf16[2,8,16,2,1536]{4,3,2,1,0:T(2,128)(2,1)} %collective-permute-done.6), kind=kLoop, calls=%fused_computation.41 | loop fusion | bytes 3145728
  134.0 7.1 %gather_fusion = bf16[8,2,16,2,1536]{4,3,2,1,0:T(2,128)(2,1)S(1)} fusion(bf16[5,2,8,16,2,1536]{5,4,3,2,1,0:T(2,128)(2,1)} %bitcast_dynamic-update-slice_fusion, s32[8]{0:T(128)S(1)} %fusion.53), kind=kCustom, calls=%fused_computation | custom fusion | bytes 3145792 | tf_op jit(solution)/shard_map/gather | solution.py:120
  143.4 2.6 %reshape_reshape_squeeze.14 = bf16[256,3,4,128]{3,2,1,0:T(4,128)(2,1)S(1)} reshape(bf16[8,1,16,2,1536]{4,3,2,1,0:T(2,128)(2,1)} %get-tuple-element.148) | data formatting | bytes 1572864 | tf_op jit(solution)/shard_map/reshape;reshape;squeeze | solution.py:49
  147.5 6.4 %while.23 = (s32[]{:T(128)}, f32[3,128,4,128]{1,3,2,0:T(8,128)}, bf16[3,256,4,128]{3,2,0,1:T(4,128)(2,1)S(1)}, bf16[3,128,4,128]{3,1,2,0:T(8,128)(2,1)S(1)}, bf1...) while((s32[]{:T(128)}, f32[3,128,4,128]{1,3,2,0:T(8,128)}, ...), condition=%wide.region_7.8_spmd.clone, body=%wide.region_4.7_spmd.clone.sunk | while | flops 68090880 | bytes 4075357 | solution.py:69
  153.9 17.6 %collective-permute-done.2 = bf16[2,4,48,2,1536]{4,3,2,1,0:T(2,128)(2,1)} collective-permute-done((bf16[2,4,48,2,1536]{4,3,2,1,0:T(2,128)(2,1)}, bf16[2,4,48,2,1536]{4,3,2,1,0:T(2,128)(2,1)}, u32[]{:S(2)}, u32[]{:S(2)}) %collective-permute-start.2) | collective-permute-done | bytes 2359328 | tf_op jit(solution)/shard_map/ppermute | solution.py:28
  171.7 9.8 %pad_maximum_fusion = bf16[2,4,48,6,1536]{4,3,2,1,0:T(8,128)(2,1)S(1)} fusion(bf16[2,4,48,2,1536]{4,3,2,1,0:T(2,128)(2,1)} %collective-permute-done.3, bf16[2,4,16,2,1536]{4,3,2,1,0:T(2,128)(2,1)} %copy-done.5, bf16[1,4,16,2,1536]{4,3,2,1,0:T(2,128)(2,1)S(1)} %bitcast.128, bf16[1,4,16,2,1536]{4,3,2,1,0:T(2,128)(2,1)} %bitcast.130, ...), kind=kLoop, calls=%fused_computation.38 | loop fusion | flops 42467328 | bytes 14155776 | tf_op jit(solution)/shard_map/concatenate | solution.py:32
  181.5 4.3 %fusion.56 = (bf16[1,4,48,6,1536]{4,3,2,1,0:T(8,128)(2,1)}, bf16[1,4,48,6,1536]{4,3,2,1,0:T(8,128)(2,1)}) fusion(bf16[2,4,48,6,1536]{4,3,2,1,0:T(8,128)(2,1)S(1)} %pad_maximum_fusion), kind=kLoop, calls=%fused_computation.70 | loop fusion | bytes 14155776 | tf_op jit(solution)/shard_map/slice | solution.py:100
  185.8 7.9 %reshape_reshape_squeeze.12 = bf16[1152,3,4,128]{3,2,1,0:T(4,128)(2,1)} reshape(bf16[1,4,48,6,1536]{4,3,2,1,0:T(8,128)(2,1)} %get-tuple-element.146) | data formatting | bytes 7077888 | tf_op jit(solution)/shard_map/reshape;reshape;squeeze | solution.py:49
  193.7 8.0 %reshape_reshape_squeeze.13 = bf16[1152,3,4,128]{3,2,1,0:T(4,128)(2,1)} reshape(bf16[1,4,48,6,1536]{4,3,2,1,0:T(8,128)(2,1)} %get-tuple-element.145) | data formatting | bytes 7077888 | tf_op jit(solution)/shard_map/reshape;reshape;squeeze | solution.py:49
  202.6 32.0 %while.22 = (s32[]{:T(128)}, f32[3,128,4,128]{1,3,2,0:T(8,128)}, bf16[3,1152,4,128]{3,2,0,1:T(4,128)(2,1)}, bf16[3,128,4,128]{3,1,2,0:T(8,128)(2,1)}, bf16[3,115...) while((s32[]{:T(128)}, f32[3,128,4,128]{1,3,2,0:T(8,128)}, ...), condition=%wide.region_3.4_spmd.clone, body=%wide.region_0.3_spmd.clone.sunk | while | flops 306183168 | bytes 21642908 | solution.py:69
  202.6 2.9 %constant_dynamic-slice_fusion.6 = (bf16[1,1152,4,128]{3,2,0,1:T(4,128)(2,1)S(1)}, bf16[1,1152,4,128]{3,2,0,1:T(4,128)(2,1)}) fusion(bf16[3,1152,4,128]{3,2,0,1:T(4,128)(2,1)} %get-tuple-element.257, s32[]{:T(128)} %get-tuple-element.246, bf16[3,1152,4,128]{3,2,0,1:T(4,128)(2,1)} %get-tuple-element.255), kind=kLoop, calls=%fused_computation.18.clone.1 | loop fusion | bytes 4718596 | tf_op jit(solution)/shard_map/while/body/jit(dynamic_index_in_dim)/dynamic_slice | solution.py:69
  213.3 2.9 %constant_dynamic-slice_fusion.6 = (bf16[1,1152,4,128]{3,2,0,1:T(4,128)(2,1)S(1)}, bf16[1,1152,4,128]{3,2,0,1:T(4,128)(2,1)}) fusion(bf16[3,1152,4,128]{3,2,0,1:T(4,128)(2,1)} %get-tuple-element.257, s32[]{:T(128)} %get-tuple-element.246, bf16[3,1152,4,128]{3,2,0,1:T(4,128)(2,1)} %get-tuple-element.255), kind=kLoop, calls=%fused_computation.18.clone.1 | loop fusion | bytes 4718596 | tf_op jit(solution)/shard_map/while/body/jit(dynamic_index_in_dim)/dynamic_slice | solution.py:69
  221.4 2.6 %fusion.72 = f32[3,128,4,128]{1,3,2,0:T(8,128)} fusion(f32[3,128,4,128]{1,3,2,0:T(8,128)} %get-tuple-element.247, s32[]{:T(128)} %get-tuple-element.246, f32[4,128,1152]{2,1,0:T(8,128)S(1)} %get-tuple-element.226, f32[4,128]{1,0:T(4,128)S(1)} %get-tuple-element.227, bf16[1,1152,4,128]{1,3,2,0:T(8,128)(2,1)} %copy.34, f32[128,4]{0,1:T(4,128)S(1)} %bitcast.134), kind=kOutput, calls=%fused_computation.15.clone.1 | convolution fusion | flops 152240128 | bytes 3805696 | tf_op jit(solution)/shard_map/while/body/eval_jaxpr/gqk,kgd->qgd/dot_general | solution.py:61
  224.0 2.9 %constant_dynamic-slice_fusion.6 = (bf16[1,1152,4,128]{3,2,0,1:T(4,128)(2,1)S(1)}, bf16[1,1152,4,128]{3,2,0,1:T(4,128)(2,1)}) fusion(bf16[3,1152,4,128]{3,2,0,1:T(4,128)(2,1)} %get-tuple-element.257, s32[]{:T(128)} %get-tuple-element.246, bf16[3,1152,4,128]{3,2,0,1:T(4,128)(2,1)} %get-tuple-element.255), kind=kLoop, calls=%fused_computation.18.clone.1 | loop fusion | bytes 4718596 | tf_op jit(solution)/shard_map/while/body/jit(dynamic_index_in_dim)/dynamic_slice | solution.py:69
  (84 shorter events, 46.4 us)
Async XLA Ops:
  0.0 27.6 %copy-start.3 = (bf16[4,16,2,1536]{3,2,1,0:T(2,128)(2,1)S(1)}, bf16[4,16,2,1536]{3,2,1,0:T(2,128)(2,1)}, u32[]{:S(2)}) copy-start(bf16[4,16,2,1536]{3,2,1,0:T(2,128)(2,1)} %param.11) | copy-start | bytes 1179652
  0.0 27.6 %copy-start.2 = (bf16[4,16,2,1536]{3,2,1,0:T(2,128)(2,1)S(1)}, bf16[4,16,2,1536]{3,2,1,0:T(2,128)(2,1)}, u32[]{:S(2)}) copy-start(bf16[4,16,2,1536]{3,2,1,0:T(2,128)(2,1)} %param.12) | copy-start | bytes 1179652
  0.0 22.3 %copy-start.7 = (s32[1,1,8]{2,1,0:T(1,128)S(1)}, s32[1,1,8]{2,1,0:T(1,128)}, u32[]{:S(2)}) copy-start(s32[1,1,8]{2,1,0:T(1,128)} %param.14) | copy-start | bytes 100
  3.3 19.0 %collective-permute-start = (bf16[2,4,16,2,1536]{4,3,2,1,0:T(2,128)(2,1)}, bf16[2,4,16,2,1536]{4,3,2,1,0:T(2,128)(2,1)S(1)}, u32[]{:S(2)}, u32[]{:S(2)}) collective-permute-start(bf16[2,4,16,2,1536]{4,3,2,1,0:T(2,128)(2,1)} %pad_maximum_fusion.2), channel_id=1, source_target_pairs={{0,1},{1,2},{2,3},{4,5},{5,6},{6,7},{8,9},{9,10},{10,11},{12,13},{... | collective-permute-start | bytes 2359304 | tf_op jit(solution)/shard_map/ppermute | solution.py:19
  7.8 19.9 %collective-permute-start.1 = (bf16[2,4,16,2,1536]{4,3,2,1,0:T(2,128)(2,1)}, bf16[2,4,16,2,1536]{4,3,2,1,0:T(2,128)(2,1)S(1)}, u32[]{:S(2)}, u32[]{:S(2)}) collective-permute-start(bf16[2,4,16,2,1536]{4,3,2,1,0:T(2,128)(2,1)} %pad_maximum_fusion.2), channel_id=1, source_target_pairs={{1,0},{2,1},{3,2},{5,4},{6,5},{7,6},{9,8},{10,9},{11,10},{13,12},{... | collective-permute-start | bytes 2359304 | tf_op jit(solution)/shard_map/ppermute | solution.py:19
  9.8 79.1 %collective-permute-start.4 = (bf16[2,8,16,2,1536]{4,3,2,1,0:T(2,128)(2,1)}, bf16[2,8,16,2,1536]{4,3,2,1,0:T(2,128)(2,1)}, u32[]{:S(2)}, u32[]{:S(2)}) collective-permute-start(bf16[2,8,16,2,1536]{4,3,2,1,0:T(2,128)(2,1)} %param.13), channel_id=1, source_target_pairs={{248,0},{252,4},{0,8},{4,12},{8,16},{12,20},{16,24},{20,28},{24,32... | collective-permute-start | bytes 4718600 | tf_op jit(solution)/shard_map/ppermute | solution.py:39
  12.8 109.1 %collective-permute-start.5 = (bf16[2,8,16,2,1536]{4,3,2,1,0:T(2,128)(2,1)}, bf16[2,8,16,2,1536]{4,3,2,1,0:T(2,128)(2,1)}, u32[]{:S(2)}, u32[]{:S(2)}) collective-permute-start(bf16[2,8,16,2,1536]{4,3,2,1,0:T(2,128)(2,1)} %param.13), channel_id=1, source_target_pairs={{252,0},{0,4},{4,8},{8,12},{12,16},{16,20},{20,24},{24,28},{28,32}... | collective-permute-start | bytes 4718600 | tf_op jit(solution)/shard_map/ppermute | solution.py:39
  14.4 113.5 %collective-permute-start.6 = (bf16[2,8,16,2,1536]{4,3,2,1,0:T(2,128)(2,1)}, bf16[2,8,16,2,1536]{4,3,2,1,0:T(2,128)(2,1)}, u32[]{:S(2)}, u32[]{:S(2)}) collective-permute-start(bf16[2,8,16,2,1536]{4,3,2,1,0:T(2,128)(2,1)} %param.13), channel_id=1, source_target_pairs={{4,0},{8,4},{12,8},{16,12},{20,16},{24,20},{28,24},{32,28},{36,32}... | collective-permute-start | bytes 4718600 | tf_op jit(solution)/shard_map/ppermute | solution.py:39
  22.3 9.8 %copy-start.4 = (bf16[2,4,16,2,1536]{4,3,2,1,0:T(2,128)(2,1)}, bf16[2,4,16,2,1536]{4,3,2,1,0:T(2,128)(2,1)S(1)}, u32[]{:S(2)}) copy-start(bf16[2,4,16,2,1536]{4,3,2,1,0:T(2,128)(2,1)S(1)} %collective-permute-done) | copy-start | bytes 2359300
  22.3 109.3 %collective-permute-start.7 = (bf16[2,8,16,2,1536]{4,3,2,1,0:T(2,128)(2,1)}, bf16[2,8,16,2,1536]{4,3,2,1,0:T(2,128)(2,1)S(1)}, u32[]{:S(2)}, u32[]{:S(2)}) collective-permute-start(bf16[2,8,16,2,1536]{4,3,2,1,0:T(2,128)(2,1)} %param.13), channel_id=1, source_target_pairs={{8,0},{12,4},{16,8},{20,12},{24,16},{28,20},{32,24},{36,28},{40,32... | collective-permute-start | bytes 4718600 | tf_op jit(solution)/shard_map/ppermute | solution.py:39
  27.7 4.4 %copy-start.5 = (bf16[2,4,16,2,1536]{4,3,2,1,0:T(2,128)(2,1)}, bf16[2,4,16,2,1536]{4,3,2,1,0:T(2,128)(2,1)S(1)}, u32[]{:S(2)}) copy-start(bf16[2,4,16,2,1536]{4,3,2,1,0:T(2,128)(2,1)S(1)} %collective-permute-done.1) | copy-start | bytes 2359300
  32.1 93.5 %copy-start.6 = (bf16[2,8,16,2,1536]{4,3,2,1,0:T(2,128)(2,1)S(1)}, bf16[2,8,16,2,1536]{4,3,2,1,0:T(2,128)(2,1)}, u32[]{:S(2)}) copy-start(bf16[2,8,16,2,1536]{4,3,2,1,0:T(2,128)(2,1)} %param.13) | copy-start | bytes 4718596
  32.1 139.5 %collective-permute-start.2 = (bf16[2,4,48,2,1536]{4,3,2,1,0:T(2,128)(2,1)}, bf16[2,4,48,2,1536]{4,3,2,1,0:T(2,128)(2,1)}, u32[]{:S(2)}, u32[]{:S(2)}) collective-permute-start(bf16[2,4,48,2,1536]{4,3,2,1,0:T(2,128)(2,1)} %pad_maximum_fusion.1), channel_id=1, source_target_pairs={{0,4},{4,8},{8,12},{12,16},{16,20},{20,24},{24,28},{28,32},{32,36}... | collective-permute-start | bytes 7077896 | tf_op jit(solution)/shard_map/ppermute | solution.py:28
  88.8 82.9 %collective-permute-start.3 = (bf16[2,4,48,2,1536]{4,3,2,1,0:T(2,128)(2,1)}, bf16[2,4,48,2,1536]{4,3,2,1,0:T(2,128)(2,1)}, u32[]{:S(2)}, u32[]{:S(2)}) collective-permute-start(bf16[2,4,48,2,1536]{4,3,2,1,0:T(2,128)(2,1)} %pad_maximum_fusion.1), channel_id=1, source_target_pairs={{4,0},{8,4},{12,8},{16,12},{20,16},{24,20},{28,24},{32,28},{36,32}... | collective-permute-start | bytes 7077896 | tf_op jit(solution)/shard_map/ppermute | solution.py:31
  153.9 17.6 %copy-start.1 = (bf16[3,128,4,128]{3,1,2,0:T(8,128)(2,1)}, bf16[3,128,4,128]{3,1,2,0:T(8,128)(2,1)S(1)}, u32[]{:S(2)}) copy-start(bf16[3,128,4,128]{3,1,2,0:T(8,128)(2,1)S(1)} %get-tuple-element.281) | copy-start | bytes 1179652
  207.4 1.3 copy-start
  218.0 1.3 copy-start
  228.7 1.3 copy-start
where the time goes:
time: 239 us; the launch traced here: 237 us
  waiting for transfers between devices  102 us (43%)
  local copies, waits for them, and re-layouts  72.5 us (30%)
  starting transfers between devices  24.4 us (10%)
  other arithmetic  21.3 us (9%)
  matrix products  16.4 us (7%)
    ppermute x4, waiting for transfers between devices, passed_along(): return lax.ppermute(block, axis, route)  83.9 us
    another operation x5, local copies, waits for them, and re-layouts, split_heads(): matrix.reshape(matrix.shape[0], blocks, group_size, HEAD_DIM)  20.3 us
    ppermute x1, waiting for transfers between devices, extended(): lax.ppermute(lax.slice_in_dim(block, block.shape[dim] - width, None, axis...  17.6 us
    dynamic_slice x12, local copies, waits for them, and re-layouts, attend(): lax.map(one_block, (split_heads(query_rows), split_heads(key_rows), split...  16.2 us
    ppermute x4, starting transfers between devices, passed_along(): return lax.ppermute(block, axis, route)  15.7 us
    unnamed x19, local copies, waits for them, and re-layouts  13.6 us
    dot_general x6, matrix products, one_block(): jnp.einsum('gqk,kgd->qgd', weights.astype(jnp.bfloat16), value_part, pref...  10.8 us
    concatenate x1, other arithmetic, extended(): block = jnp.concatenate([low, block, high], axis=dim)  9.8 us
  transfers between devices with their start and end apart: 8, of which 4 were waited for; matrix products, arithmetic and copies ran while one was open for 18% of the time, Pallas kernels for 0%

commit v1 on v0

v1 whole, which is shorter than its diff:
```python
import functools

import jax
import jax.numpy as jnp
from jax import lax
from jax.experimental import pallas as pl
from jax.experimental.pallas import tpu as pltpu
from jax.sharding import PartitionSpec as P

HEAD_DIM = 128
REACH = 2
MASKED = -1e30
FLOOR = -30000.0
SCALE2 = HEAD_DIM ** (-0.5) * 1.4426950408889634
FAR_LANE = 36
LOW_LANE = 12
EXP_LANE = 24
STAT = 128
CODE_ROWS = 16

VMEM = pl.BlockSpec(memory_space=pltpu.VMEM)
SMEM = pl.BlockSpec(memory_space=pltpu.SMEM)
ANY = pl.BlockSpec(memory_space=pl.ANY)
PARAMS = pltpu.CompilerParams(vmem_limit_bytes=48 * 1024 * 1024)


def call(body, out_shape, in_specs, *operands):
    single = not isinstance(out_shape, (list, tuple))
    return pl.pallas_call(
        body,
        out_shape=out_shape,
        in_specs=in_specs,
        out_specs=VMEM if single else [VMEM] * len(out_shape),
        compiler_params=PARAMS,
    )(*operands)


def columns(head):
    return pl.ds(head * HEAD_DIM, HEAD_DIM)


def dot_t(a, b):
    return lax.dot_general(a, b, (((1,), (1,)), ((), ())), preferred_element_type=jnp.float32)


def prep_queries(q_ref, ids_ref, count_ref, out_ref, *, slots, sectors):
    rows = q_ref.shape[0] * q_ref.shape[1] * q_ref.shape[2]
    width = q_ref.shape[3]
    out_ref[:rows, :] = q_ref[...].reshape(rows, width)
    sector = lax.axis_index("lon")
    block = q_ref.shape[1] * q_ref.shape[2]
    lane_code = lax.broadcasted_iota(jnp.int32, (CODE_ROWS, width), 1) // block
    live = count_ref[0, 0]
    bias = jnp.full((CODE_ROWS, width), MASKED, jnp.float32)
    for e in range(ids_ref.shape[2]):
        entry = ids_ref[0, 0, e]
        owner = entry // slots
        offset = lax.rem(owner - sector + REACH + sectors, sectors)
        code = jnp.where(e < live, offset * slots + entry % slots, -1)
        bias = jnp.where(lane_code == code, 0.0, bias)
    out_ref[rows:, :] = bias.astype(jnp.bfloat16)


def prep_pair(k_ref, v_ref, out_ref):
    rows = out_ref.shape[0] // 2
    out_ref[:rows, :] = k_ref[...].reshape(rows, out_ref.shape[1])
    out_ref[rows:, :] = v_ref[...].reshape(rows, out_ref.shape[1])


def prep_bank(bank_ref, out_ref):
    out_ref[...] = bank_ref[...].reshape(out_ref.shape)


def softmax_part(scores, values):
    largest = jnp.max(scores, axis=1, keepdims=True)
    weights = jnp.exp2((scores - largest) * SCALE2)
    total = jnp.sum(weights, axis=1, keepdims=True)
    mixed = jnp.dot(weights.astype(jnp.bfloat16), values, preferred_element_type=jnp.float32)
    level = jnp.maximum(largest * SCALE2 + jnp.log2(total), FLOOR)
    return mixed * (1.0 / total), level


def near_part(queries, tiles, head):
    band = lax.axis_index("lat")
    bands = lax.axis_size("lat")
    rows = tiles[0].shape[0] // 2
    shut = (
        None,
        jnp.where(band > 0, 0.0, MASKED).astype(jnp.float32),
        jnp.where(band < bands - 1, 0.0, MASKED).astype(jnp.float32),
    )
    scores, values = [], []
    for tile, closed in zip(tiles, shut):
        part = dot_t(queries, tile[:rows, columns(head)])
        scores.append(part if closed is None else part + closed)
        values.append(tile[rows:, columns(head)])
    return softmax_part(jnp.concatenate(scores, axis=1), jnp.concatenate(values, axis=0))


def far_part(queries, biases, bank, head):
    rows = bank.shape[0] // 2
    scores = dot_t(queries, bank[:rows, columns(head)])
    each = scores.shape[0] // len(biases)
    scores = jnp.concatenate(
        [scores[i * each : (i + 1) * each] + bias for i, bias in enumerate(biases)], axis=0
    )
    return softmax_part(scores, bank[rows:, columns(head)])


def mask_of(q_ref, offset, keys):
    rows = q_ref.shape[0] - CODE_ROWS
    return q_ref[rows:, pl.ds((offset + REACH) * keys, keys)].astype(jnp.float32)[:1]


def put_coded(out_ref, stats, lanes, mixed, level, column, lane):
    peak = jnp.max(jnp.abs(mixed), axis=1, keepdims=True)
    power = jnp.ceil(jnp.log2(jnp.maximum(peak, 1e-30)))
    out_ref[:, columns(column)] = jnp.round(mixed * jnp.exp2(14.0 - power)).astype(jnp.int32).astype(jnp.int16)
    whole = jnp.floor(level)
    low = jnp.minimum(jnp.floor((level - whole) * 32768.0), 32767.0)
    stats = jnp.where(lanes == lane, whole, stats)
    stats = jnp.where(lanes == lane + LOW_LANE, low, stats)
    return jnp.where(lanes == lane + EXP_LANE, power, stats)


def part_near_far(low_ref, high_ref, own_ref, up_ref, down_ref, bank_ref, low_out, high_out):
    rows = low_out.shape[0]
    heads = own_ref.shape[1] // HEAD_DIM
    keys = bank_ref.shape[0] // 2
    lanes = lax.broadcasted_iota(jnp.int32, (rows, STAT), 1)
    biases = [mask_of(low_ref, 1, keys), mask_of(high_ref, -1, keys)]
    outs = (low_out, high_out)
    stats = [jnp.zeros((rows, STAT), jnp.float32) for _ in outs]
    for head in range(heads):
        queries = jnp.concatenate([low_ref[:rows, columns(head)], high_ref[:rows, columns(head)]], axis=0)
        near, near_level = near_part(queries, (own_ref, up_ref, down_ref), head)
        far, far_level = far_part(queries, biases, bank_ref, head)
        for i, out in enumerate(outs):
            cut = slice(i * rows, (i + 1) * rows)
            stats[i] = put_coded(out, stats[i], lanes, near[cut], near_level[cut], head, head)
            stats[i] = put_coded(
                out, stats[i], lanes, far[cut], far_level[cut], heads + head, FAR_LANE + head
            )
    for out, stat in zip(outs, stats):
        out[:, 2 * heads * HEAD_DIM :] = stat.astype(jnp.int32).astype(jnp.int16)


def part_far(low_ref, high_ref, bank_ref, low_out, high_out):
    rows = low_out.shape[0]
    heads = bank_ref.shape[1] // HEAD_DIM
    keys = bank_ref.shape[0] // 2
    lanes = lax.broadcasted_iota(jnp.int32, (rows, STAT), 1)
    biases = [mask_of(low_ref, 2, keys), mask_of(high_ref, -2, keys)]
    outs = (low_out, high_out)
    stats = [jnp.where(lanes < FAR_LANE, FLOOR, 0.0) for _ in outs]
    for head in range(heads):
        queries = jnp.concatenate([low_ref[:rows, columns(head)], high_ref[:rows, columns(head)]], axis=0)
        far, far_level = far_part(queries, biases, bank_ref, head)
        for i, out in enumerate(outs):
            cut = slice(i * rows, (i + 1) * rows)
            stats[i] = put_coded(out, stats[i], lanes, far[cut], far_level[cut], head, FAR_LANE + head)
    for out, stat in zip(outs, stats):
        out[:, heads * HEAD_DIM :] = stat.astype(jnp.int32).astype(jnp.int16)


def part_own(q_ref, own_ref, up_ref, down_ref, bank_ref, _after, near_out, far_out, level_out):
    rows = near_out.shape[0]
    heads = own_ref.shape[1] // HEAD_DIM
    keys = bank_ref.shape[0] // 2
    lanes = lax.broadcasted_iota(jnp.int32, (rows, STAT), 1)
    bias = mask_of(q_ref, 0, keys)
    levels = jnp.full((rows, STAT), FLOOR, jnp.float32)
    for head in range(heads):
        queries = q_ref[:rows, columns(head)]
        near, near_level = near_part(queries, (own_ref, up_ref, down_ref), head)
        far, far_level = far_part(queries, [bias], bank_ref, head)
        near_out[:, columns(head)] = near
        far_out[:, columns(head)] = far
        levels = jnp.where(lanes == head, near_level, levels)
        levels = jnp.where(lanes == FAR_LANE + head, far_level, levels)
    level_out[...] = levels


def merge(near_ref, far_ref, level_ref, one_low, one_high, two_low, two_high, out_ref):
    rows, width = near_ref.shape
    heads = width // HEAD_DIM
    near_far = (one_low, one_high)
    far_only = (two_low, two_high)
    levels, factors = [level_ref[...]], [None]
    for ref in near_far + far_only:
        stat = ref[:, ref.shape[1] - STAT :].astype(jnp.int32).astype(jnp.float32)
        low = pltpu.roll(stat, STAT - LOW_LANE, 1)
        power = pltpu.roll(stat, STAT - EXP_LANE, 1)
        levels.append(stat + low * (1.0 / 32768.0))
        factors.append(jnp.exp2(power - 14.0))
    lanes = lax.broadcasted_iota(jnp.int32, (rows, STAT), 1)
    for i in (3, 4):
        levels[i] = jnp.where(lanes < FAR_LANE, FLOOR, levels[i])
    largest = functools.reduce(jnp.maximum, levels)
    weights = [jnp.exp2(level - largest) for level in levels]
    inverse = 1.0 / functools.reduce(jnp.add, weights)
    shares = [w * inverse if f is None else w * inverse * f for w, f in zip(weights, factors)]

    def decoded(ref, column):
        return ref[:, columns(column)].astype(jnp.int32).astype(jnp.float32)

    for head in range(heads):
        near, far = slice(head, head + 1), slice(FAR_LANE + head, FAR_LANE + head + 1)
        total = near_ref[:, columns(head)] * shares[0][:, near] + far_ref[:, columns(head)] * shares[0][:, far]
        for ref, share in zip(near_far, shares[1:3]):
            total += decoded(ref, head) * share[:, near] + decoded(ref, heads + head) * share[:, far]
        for ref, share in zip(far_only, shares[3:]):
            total += decoded(ref, head) * share[:, far]
        out_ref[:, :, :, columns(head)] = total.astype(jnp.bfloat16).reshape(out_ref.shape[:3] + (HEAD_DIM,))


def around(value, steps):
    count = lax.axis_size("lon")
    return lax.ppermute(value, "lon", [(i, (i + steps) % count) for i in range(count)])


def along(value, steps):
    count = lax.axis_size("lat")
    return lax.ppermute(
        value, "lat", [(i, i + steps) for i in range(count) if 0 <= i + steps < count]
    )


def local(queries, token_keys, token_values, memory_bank, memory_ids, memory_count):
    frames, band_rows, tile_cols, width = queries.shape
    rows = frames * band_rows * tile_cols
    slots = memory_bank.shape[1]
    sectors = lax.axis_size("lon")
    shape = jax.ShapeDtypeStruct

    coded_queries = call(
        functools.partial(prep_queries, slots=slots, sectors=sectors),
        shape((rows + CODE_ROWS, width), jnp.bfloat16),
        [VMEM, SMEM, SMEM],
        queries, memory_ids, memory_count,
    )
    one_low, one_high = around(coded_queries, 1), around(coded_queries, -1)
    pair = call(prep_pair, shape((2 * rows, width), jnp.bfloat16), [VMEM, VMEM], token_keys, token_values)
    up, down = along(pair, 1), along(pair, -1)
    bank = call(
        prep_bank,
        shape((2 * slots * band_rows * tile_cols, width), jnp.bfloat16),
        [VMEM], memory_bank,
    )
    two_low, two_high = around(one_low, 1), around(one_high, -1)
    both = shape((rows, 2 * width + STAT), jnp.int16)
    single = shape((rows, width + STAT), jnp.int16)
    one_low_out, one_high_out = call(
        part_near_far, [both, both], [VMEM] * 6, one_low, one_high, pair, up, down, bank
    )
    back_one_high = around(one_low_out, -1)
    back_one_low = around(one_high_out, 1)
    two_low_out, two_high_out = call(part_far, [single, single], [VMEM] * 3, two_low, two_high, bank)
    back_two_high = around(two_low_out, -2)
    back_two_low = around(two_high_out, 2)
    near, far, level = call(
        part_own,
        [shape((rows, width), jnp.float32)] * 2 + [shape((rows, STAT), jnp.float32)],
        [VMEM] * 5 + [ANY],
        coded_queries, pair, up, down, bank, two_low_out,
    )
    return call(
        merge, shape(queries.shape, jnp.bfloat16), [VMEM] * 7,
        near, far, level, back_one_low, back_one_high, back_two_low, back_two_high,
    )


def solution(mesh):
    placed = (
        P(None, "lat", "lon", None),
        P(None, "lat", "lon", None),
        P(None, "lat", "lon", None),
        P(None, None, "lat", "lon", None),
        P("lat", "lon", None),
        P("lat", "lon"),
    )
    return jax.shard_map(
        local, mesh=mesh, in_specs=placed, out_specs=P(None, "lat", "lon", None), check_vma=False
    )
```

time: 239 us -> 96.8 us (0.41)
  waiting for transfers between devices: 102 us -> 28.5 us
  local copies, waits for them, and re-layouts: 72.5 us -> 3.87 us
  Pallas kernels: 0 us -> 22.9 us
  other arithmetic: 21.3 us -> 0 us
  matrix products: 16.4 us -> 0 us
  starting transfers between devices: 24.4 us -> 40.6 us
    ppermute x8 -> x10, waiting for transfers between devices: 102 us -> 28.5 us  [the longest x8 28.5 us: around(): lax.ppermute(value, 'lon', [(i, (i + steps) % count) for i in range(count)])]
    another operation x9 -> x0, local copies, waits for them, and re-layouts: 24.5 us -> none  [the longest x5 20.3 us: split_heads(): matrix.reshape(matrix.shape[0], blocks, group_size, HEAD_DIM)]
    pallas_call x0 -> x7, Pallas kernels: none -> 22.9 us  [call(): pl.pallas_call(body, out_shape=out_shape, in_specs=in_specs, out_specs=VM...]
    dot_general x12 -> x0, matrix products: 16.4 us -> none  [the longest x6 10.8 us: one_block(): jnp.einsum('gqk,kgd->qgd', weights.astype(jnp.bfloat16), value_part, pref...]
    dynamic_slice x12 -> x0, local copies, waits for them, and re-layouts: 16.2 us -> none  [attend(): lax.map(one_block, (split_heads(query_rows), split_heads(key_rows), split...]
    ppermute x8 -> x10, starting transfers between devices: 24.4 us -> 40.6 us  [the longest x8 33.4 us: around(): lax.ppermute(value, 'lon', [(i, (i + steps) % count) for i in range(count)])]
    concatenate x4 -> x0, other arithmetic: 14.3 us -> none  [the longest x1 9.8 us: extended(): block = jnp.concatenate([low, block, high], axis=dim)]
    unnamed x19 -> x14, local copies, waits for them, and re-layouts: 13.6 us -> 3.87 us
  transfers between devices with their start and end apart: 8 -> 10, of which waited for: 4 -> 2; matrix products, arithmetic and copies ran while one was open for 18% -> 0% of each run, Pallas kernels for 0% -> 21%
where the time goes in v1:
time: 96.8 us; the launch traced here: 96.6 us
  starting transfers between devices  40.6 us (42%)
  waiting for transfers between devices  28.5 us (29%)
  Pallas kernels  22.9 us (24%)
  local copies, waits for them, and re-layouts  3.87 us (4%)
    ppermute x8, starting transfers between devices, around(): lax.ppermute(value, 'lon', [(i, (i + steps) % count) for i in range(count)])  33.4 us
    ppermute x8, waiting for transfers between devices, around(): lax.ppermute(value, 'lon', [(i, (i + steps) % count) for i in range(count)])  28.5 us
    pallas_call x7, Pallas kernels, call(): pl.pallas_call(body, out_shape=out_shape, in_specs=in_specs, out_specs=VM...  22.9 us
    ppermute x2, starting transfers between devices, along(): lax.ppermute(value, 'lat', [(i, i + steps) for i in range(count) if 0 <=...  7.2 us
    unnamed x14, local copies, waits for them, and re-layouts  3.87 us
  transfers between devices with their start and end apart: 10, of which 2 were waited for; matrix products, arithmetic and copies ran while one was open for 0% of the time, Pallas kernels for 21%

profile of v1, /device:TPU:1, one launch (start us, length us, event | category | flops | bytes accessed | tf_op | source)
XLA Modules:
  0.0 96.6 jit_solution(14942666315232379785)
XLA Ops:
  0.0 1.0 %copy-done.4 = bf16[4,16,2,1536]{3,2,1,0:T(2,128)(2,1)S(1)} copy-done((bf16[4,16,2,1536]{3,2,1,0:T(2,128)(2,1)S(1)}, bf16[4,16,2,1536]{3,2,1,0:T(2,128)(2,1)}, u32[]{:S(2)}) %copy-start.4) | copy-done | bytes 393240
  1.1 1.0 %copy-done.5 = bf16[4,16,2,1536]{3,2,1,0:T(2,128)(2,1)S(1)} copy-done((bf16[4,16,2,1536]{3,2,1,0:T(2,128)(2,1)S(1)}, bf16[4,16,2,1536]{3,2,1,0:T(2,128)(2,1)}, u32[]{:S(2)}) %copy-start.5) | copy-done | bytes 393240
  2.0 0.1 shard_map.65.own_ref
  2.1 5.3 %collective-permute-start.1 = (bf16[256,1536]{1,0:T(8,128)(2,1)S(1)}, bf16[256,1536]{1,0:T(8,128)(2,1)S(1)}, u32[]{:S(2)}, u32[]{:S(2)}) collective-permute-start(bf16[256,1536]{1,0:T(8,128)(2,1)S(1)} %shard_map.65.own_ref), channel_id=1, source_target_pairs={{1,0},{2,1},{3,2},{5,4},{6,5},{7,6},{9,8},{10,9},{11,10},{13,12},{... | collective-permute-start | bytes 2359304 | tf_op jit(solution)/shard_map/ppermute | solution.py:224
  7.4 1.9 %collective-permute-start = (bf16[256,1536]{1,0:T(8,128)(2,1)S(1)}, bf16[256,1536]{1,0:T(8,128)(2,1)S(1)}, u32[]{:S(2)}, u32[]{:S(2)}) collective-permute-start(bf16[256,1536]{1,0:T(8,128)(2,1)S(1)} %shard_map.65.own_ref), channel_id=1, source_target_pairs={{0,1},{1,2},{2,3},{4,5},{5,6},{6,7},{8,9},{9,10},{10,11},{12,13},{... | collective-permute-start | bytes 2359304 | tf_op jit(solution)/shard_map/ppermute | solution.py:224
  10.0 0.0 copy-start.6
  10.0 0.6 copy-done.6
  10.7 0.7 shard_map.64.q_ref
  11.3 9.9 %collective-permute-start.4 = (bf16[144,1536]{1,0:T(8,128)(2,1)S(1)}, bf16[144,1536]{1,0:T(8,128)(2,1)S(1)}, u32[]{:S(2)}, u32[]{:S(2)}) collective-permute-start(bf16[144,1536]{1,0:T(8,128)(2,1)S(1)} %shard_map.64.q_ref), channel_id=1, source_target_pairs={{0,252},{4,0},{8,4},{12,8},{16,12},{20,16},{24,20},{28,24},{32,28}... | collective-permute-start | bytes 1327112 | tf_op jit(solution)/shard_map/ppermute | solution.py:219
  21.2 0.0 collective-permute-start.2
  21.2 10.0 %collective-permute-done.4.high_ref = bf16[144,1536]{1,0:T(8,128)(2,1)S(1)} collective-permute-done((bf16[144,1536]{1,0:T(8,128)(2,1)S(1)}, bf16[144,1536]{1,0:T(8,128)(2,1)S(1)}, u32[]{:S(2)}, u32[]{:S(2)}) %collective-permute-start.4) | collective-permute-done | bytes 442400 | tf_op jit(solution)/shard_map/ppermute | solution.py:219
  31.2 7.8 %collective-permute-start.5 = (bf16[144,1536]{1,0:T(8,128)(2,1)S(1)}, bf16[144,1536]{1,0:T(8,128)(2,1)S(1)}, u32[]{:S(2)}, u32[]{:S(2)}) collective-permute-start(bf16[144,1536]{1,0:T(8,128)(2,1)S(1)} %collective-permute-done.4.high_ref), channel_id=1, source_target_pairs={{0,252},{4,0},{8,4},{12,8},{16,12},{20,16},{24,20},{28,24},{32,28}... | collective-permute-start | bytes 1327112 | tf_op jit(solution)/shard_map/ppermute | solution.py:219
  39.0 0.0 collective-permute-done.2.low_ref
  39.0 0.2 shard_map.66.bank_ref
  39.2 1.2 %copy-done = bf16[512,1536]{1,0:T(8,128)(2,1)} copy-done((bf16[512,1536]{1,0:T(8,128)(2,1)}, bf16[512,1536]{1,0:T(8,128)(2,1)S(1)}, u32[]{:S(2)}) %copy-start) | copy-done | bytes 1572888
  40.4 9.3 %shard_map.69 = (s16[128,3200]{1,0:T(8,128)(2,1)S(1)}, s16[128,3200]{1,0:T(8,128)(2,1)S(1)}) custom-call(bf16[144,1536]{1,0:T(8,128)(2,1)S(1)} %collective-permute-done.2.low_ref, bf16[144,1536]{1,0:T(8,128)(2,1)S(1)} %collective-permute-done.4.high_ref, bf16[256,1536]{1,0:T(8,128)(2,1)S(1)} %shard_map.65.own_ref, ...), custom_call_target="tpu_custom_call" | custom-call | tf_op jit(solution)/shard_map/pallas_call | solution.py:29
  49.7 0.1 collective-permute-start.6
  49.8 7.4 %collective-permute-start.7 = (s16[128,3200]{1,0:T(8,128)(2,1)S(1)}, s16[128,3200]{1,0:T(8,128)(2,1)S(1)}, u32[]{:S(2)}, u32[]{:S(2)}) collective-permute-start(s16[128,3200]{1,0:T(8,128)(2,1)S(1)} %get-tuple-element.17), channel_id=1, source_target_pairs={{0,252},{4,0},{8,4},{12,8},{16,12},{20,16},{24,20},{28,24},{32,28}... | collective-permute-start | bytes 2457608 | tf_op jit(solution)/shard_map/ppermute | solution.py:219
  57.2 2.4 %shard_map.67 = (s16[128,1664]{1,0:T(8,128)(2,1)S(1)}, s16[128,1664]{1,0:T(8,128)(2,1)S(1)}) custom-call(bf16[144,1536]{1,0:T(8,128)(2,1)S(1)} %collective-permute-done.3.low_ref, bf16[144,1536]{1,0:T(8,128)(2,1)S(1)} %collective-permute-done.5.high_ref, bf16[512,1536]{1,0:T(8,128)(2,1)S(1)} %copy-done.1), custom_call_target="tpu_custom_call" | custom-call | tf_op jit(solution)/shard_map/pallas_call | solution.py:29
  59.6 0.1 collective-permute-start.8
  59.7 8.1 %collective-permute-start.9 = (s16[128,1664]{1,0:T(8,128)(2,1)S(1)}, s16[128,1664]{1,0:T(8,128)(2,1)S(1)}, u32[]{:S(2)}, u32[]{:S(2)}) collective-permute-start(s16[128,1664]{1,0:T(8,128)(2,1)S(1)} %get-tuple-element.12._after), channel_id=1, source_target_pairs={{0,248},{4,252},{8,0},{12,4},{16,8},{20,12},{24,16},{28,20},{32,24... | collective-permute-start | bytes 1277960 | tf_op jit(solution)/shard_map/ppermute | solution.py:219
  67.8 7.5 %shard_map.68 = (f32[128,1536]{1,0:T(8,128)S(1)}, f32[128,1536]{1,0:T(8,128)S(1)}, f32[128,128]{1,0:T(8,128)S(1)}) custom-call(bf16[144,1536]{1,0:T(8,128)(2,1)S(1)} %shard_map.64.q_ref, bf16[256,1536]{1,0:T(8,128)(2,1)S(1)} %shard_map.65.own_ref, bf16[256,1536]{1,0:T(8,128)(2,1)S(1)} %collective-permute-done.up_ref, ...), custom_call_target="tpu_custom_call" | custom-call | tf_op jit(solution)/shard_map/pallas_call | solution.py:29
  75.2 18.5 %collective-permute-done.8.two_low = s16[128,1664]{1,0:T(8,128)(2,1)S(1)} collective-permute-done((s16[128,1664]{1,0:T(8,128)(2,1)S(1)}, s16[128,1664]{1,0:T(8,128)(2,1)S(1)}, u32[]{:S(2)}, u32[]{:S(2)}) %collective-permute-start.8) | collective-permute-done | bytes 426016 | tf_op jit(solution)/shard_map/ppermute | solution.py:219
  93.7 2.9 %shard_map.70 = bf16[4,16,2,1536]{3,2,1,0:T(2,128)(2,1)} custom-call(f32[128,1536]{1,0:T(8,128)S(1)} %get-tuple-element.13.near_ref, f32[128,1536]{1,0:T(8,128)S(1)} %get-tuple-element.14.far_ref, f32[128,128]{1,0:T(8,128)S(1)} %get-tuple-element.15.level_ref, s16[128,3200]{1,0:T(8,128)(2,1)S(1)} %collective-permute-done.6.one_low, ...), custom_call_target="tpu_custom_call" | custom-call | tf_op jit(solution)/shard_map/pallas_call | solution.py:29
  (17 shorter events, 0.0 us)
Async XLA Ops:
  0.0 10.0 %copy-start.3 = (bf16[4,16,2,1536]{3,2,1,0:T(2,128)(2,1)S(1)}, bf16[4,16,2,1536]{3,2,1,0:T(2,128)(2,1)}, u32[]{:S(2)}) copy-start(bf16[4,16,2,1536]{3,2,1,0:T(2,128)(2,1)} %q_ref.1) | copy-start | bytes 1179652
  0.0 1.0 %copy-start.4 = (bf16[4,16,2,1536]{3,2,1,0:T(2,128)(2,1)S(1)}, bf16[4,16,2,1536]{3,2,1,0:T(2,128)(2,1)}, u32[]{:S(2)}) copy-start(bf16[4,16,2,1536]{3,2,1,0:T(2,128)(2,1)} %k_ref.1) | copy-start | bytes 1179652
  1.1 1.0 %copy-start.5 = (bf16[4,16,2,1536]{3,2,1,0:T(2,128)(2,1)S(1)}, bf16[4,16,2,1536]{3,2,1,0:T(2,128)(2,1)}, u32[]{:S(2)}) copy-start(bf16[4,16,2,1536]{3,2,1,0:T(2,128)(2,1)} %v_ref.1) | copy-start | bytes 1179652
  2.0 37.0 %copy-start.2 = (bf16[2,8,16,2,1536]{4,3,2,1,0:T(2,128)(2,1)S(1)}, bf16[2,8,16,2,1536]{4,3,2,1,0:T(2,128)(2,1)}, u32[]{:S(2)}) copy-start(bf16[2,8,16,2,1536]{4,3,2,1,0:T(2,128)(2,1)} %bank_ref.1) | copy-start | bytes 4718596
  2.1 38.2 %collective-permute-start.1 = (bf16[256,1536]{1,0:T(8,128)(2,1)S(1)}, bf16[256,1536]{1,0:T(8,128)(2,1)S(1)}, u32[]{:S(2)}, u32[]{:S(2)}) collective-permute-start(bf16[256,1536]{1,0:T(8,128)(2,1)S(1)} %shard_map.65.own_ref), channel_id=1, source_target_pairs={{1,0},{2,1},{3,2},{5,4},{6,5},{7,6},{9,8},{10,9},{11,10},{13,12},{... | collective-permute-start | bytes 2359304 | tf_op jit(solution)/shard_map/ppermute | solution.py:224
  7.4 33.0 %collective-permute-start = (bf16[256,1536]{1,0:T(8,128)(2,1)S(1)}, bf16[256,1536]{1,0:T(8,128)(2,1)S(1)}, u32[]{:S(2)}, u32[]{:S(2)}) collective-permute-start(bf16[256,1536]{1,0:T(8,128)(2,1)S(1)} %shard_map.65.own_ref), channel_id=1, source_target_pairs={{0,1},{1,2},{2,3},{4,5},{5,6},{6,7},{8,9},{9,10},{10,11},{12,13},{... | collective-permute-start | bytes 2359304 | tf_op jit(solution)/shard_map/ppermute | solution.py:224
  10.0 0.7 copy-start.6
  11.3 19.9 %collective-permute-start.4 = (bf16[144,1536]{1,0:T(8,128)(2,1)S(1)}, bf16[144,1536]{1,0:T(8,128)(2,1)S(1)}, u32[]{:S(2)}, u32[]{:S(2)}) collective-permute-start(bf16[144,1536]{1,0:T(8,128)(2,1)S(1)} %shard_map.64.q_ref), channel_id=1, source_target_pairs={{0,252},{4,0},{8,4},{12,8},{16,12},{20,16},{24,20},{28,24},{32,28}... | collective-permute-start | bytes 1327112 | tf_op jit(solution)/shard_map/ppermute | solution.py:219
  21.2 17.8 %collective-permute-start.2 = (bf16[144,1536]{1,0:T(8,128)(2,1)S(1)}, bf16[144,1536]{1,0:T(8,128)(2,1)S(1)}, u32[]{:S(2)}, u32[]{:S(2)}) collective-permute-start(bf16[144,1536]{1,0:T(8,128)(2,1)S(1)} %shard_map.64.q_ref), channel_id=1, source_target_pairs={{0,4},{4,8},{8,12},{12,16},{16,20},{20,24},{24,28},{28,32},{32,36}... | collective-permute-start | bytes 1327112 | tf_op jit(solution)/shard_map/ppermute | solution.py:219
  31.2 26.0 %collective-permute-start.5 = (bf16[144,1536]{1,0:T(8,128)(2,1)S(1)}, bf16[144,1536]{1,0:T(8,128)(2,1)S(1)}, u32[]{:S(2)}, u32[]{:S(2)}) collective-permute-start(bf16[144,1536]{1,0:T(8,128)(2,1)S(1)} %collective-permute-done.4.high_ref), channel_id=1, source_target_pairs={{0,252},{4,0},{8,4},{12,8},{16,12},{20,16},{24,20},{28,24},{32,28}... | collective-permute-start | bytes 1327112 | tf_op jit(solution)/shard_map/ppermute | solution.py:219
  39.0 18.2 %collective-permute-start.3 = (bf16[144,1536]{1,0:T(8,128)(2,1)S(1)}, bf16[144,1536]{1,0:T(8,128)(2,1)S(1)}, u32[]{:S(2)}, u32[]{:S(2)}) collective-permute-start(bf16[144,1536]{1,0:T(8,128)(2,1)S(1)} %collective-permute-done.2.low_ref), channel_id=1, source_target_pairs={{0,4},{4,8},{8,12},{12,16},{16,20},{20,24},{24,28},{28,32},{32,36}... | collective-permute-start | bytes 1327112 | tf_op jit(solution)/shard_map/ppermute | solution.py:219
  39.2 1.2 %copy-start = (bf16[512,1536]{1,0:T(8,128)(2,1)}, bf16[512,1536]{1,0:T(8,128)(2,1)S(1)}, u32[]{:S(2)}) copy-start(bf16[512,1536]{1,0:T(8,128)(2,1)S(1)} %shard_map.66.bank_ref) | copy-start | bytes 4718596
  40.4 16.8 %copy-start.1 = (bf16[512,1536]{1,0:T(8,128)(2,1)S(1)}, bf16[512,1536]{1,0:T(8,128)(2,1)}, u32[]{:S(2)}) copy-start(bf16[512,1536]{1,0:T(8,128)(2,1)} %copy-done) | copy-start | bytes 4718596
  49.7 44.0 %collective-permute-start.6 = (s16[128,3200]{1,0:T(8,128)(2,1)S(1)}, s16[128,3200]{1,0:T(8,128)(2,1)S(1)}, u32[]{:S(2)}, u32[]{:S(2)}) collective-permute-start(s16[128,3200]{1,0:T(8,128)(2,1)S(1)} %get-tuple-element.16), channel_id=1, source_target_pairs={{0,4},{4,8},{8,12},{12,16},{16,20},{20,24},{24,28},{28,32},{32,36}... | collective-permute-start | bytes 2457608 | tf_op jit(solution)/shard_map/ppermute | solution.py:219
  49.8 43.9 %collective-permute-start.7 = (s16[128,3200]{1,0:T(8,128)(2,1)S(1)}, s16[128,3200]{1,0:T(8,128)(2,1)S(1)}, u32[]{:S(2)}, u32[]{:S(2)}) collective-permute-start(s16[128,3200]{1,0:T(8,128)(2,1)S(1)} %get-tuple-element.17), channel_id=1, source_target_pairs={{0,252},{4,0},{8,4},{12,8},{16,12},{20,16},{24,20},{28,24},{32,28}... | collective-permute-start | bytes 2457608 | tf_op jit(solution)/shard_map/ppermute | solution.py:219
  59.6 34.1 %collective-permute-start.8 = (s16[128,1664]{1,0:T(8,128)(2,1)S(1)}, s16[128,1664]{1,0:T(8,128)(2,1)S(1)}, u32[]{:S(2)}, u32[]{:S(2)}) collective-permute-start(s16[128,1664]{1,0:T(8,128)(2,1)S(1)} %get-tuple-element.18), channel_id=1, source_target_pairs={{0,8},{4,12},{8,16},{12,20},{16,24},{20,28},{24,32},{28,36},{32,40... | collective-permute-start | bytes 1277960 | tf_op jit(solution)/shard_map/ppermute | solution.py:219
  59.7 34.0 %collective-permute-start.9 = (s16[128,1664]{1,0:T(8,128)(2,1)S(1)}, s16[128,1664]{1,0:T(8,128)(2,1)S(1)}, u32[]{:S(2)}, u32[]{:S(2)}) collective-permute-start(s16[128,1664]{1,0:T(8,128)(2,1)S(1)} %get-tuple-element.12._after), channel_id=1, source_target_pairs={{0,248},{4,252},{8,0},{12,4},{16,8},{20,12},{24,16},{28,20},{32,24... | collective-permute-start | bytes 1277960 | tf_op jit(solution)/shard_map/ppermute | solution.py:219

commit v2 on v1

v2 whole, which is shorter than its diff:
```python
import functools

import jax
import jax.numpy as jnp
from jax import lax
from jax.experimental import pallas as pl
from jax.experimental.pallas import tpu as pltpu
from jax.sharding import PartitionSpec as P

HEAD_DIM = 128
REACH = 2
CAP = 4
MASKED = -1e30
FLOOR = -30000.0
SCALE2 = HEAD_DIM ** (-0.5) * 1.4426950408889634
FAR_LANE = 64
LOW_LANE = 12
EXP_LANE = 24
STAT = 128
CODE_ROWS = 16
ROUNDER = 12582912.0

VMEM = pl.BlockSpec(memory_space=pltpu.VMEM)
SMEM = pl.BlockSpec(memory_space=pltpu.SMEM)
ANY = pl.BlockSpec(memory_space=pl.ANY)
PARAMS = pltpu.CompilerParams(vmem_limit_bytes=48 * 1024 * 1024)


def call(body, out_shape, in_specs, *operands, scratch=()):
    single = not isinstance(out_shape, (list, tuple))
    return pl.pallas_call(
        body,
        out_shape=out_shape,
        in_specs=in_specs,
        out_specs=VMEM if single else [VMEM] * len(out_shape),
        scratch_shapes=list(scratch),
        compiler_params=PARAMS,
    )(*operands)


def columns(head):
    return pl.ds(head * HEAD_DIM, HEAD_DIM)


def dot_t(a, b):
    return lax.dot_general(a, b, (((1,), (1,)), ((), ())), preferred_element_type=jnp.float32)


def prep_queries(q_ref, ids_ref, out_ref, *, slots, sectors):
    rows = q_ref.shape[0] * q_ref.shape[1] * q_ref.shape[2]
    width = q_ref.shape[3]
    out_ref[:rows, :] = q_ref[...].reshape(rows, width)
    sector = lax.axis_index("lon")
    block = q_ref.shape[1] * q_ref.shape[2]
    lane_code = lax.broadcasted_iota(jnp.int32, (CODE_ROWS, width), 1) // block
    bias = jnp.full((CODE_ROWS, width), MASKED, jnp.float32)
    used = [jnp.int32(0), jnp.int32(0)]
    for e in range(ids_ref.shape[0]):
        entry = ids_ref[e]
        offset = lax.rem(entry // slots - sector + REACH + sectors, sectors)
        place = entry % slots
        for i, far_end in enumerate((0, 2 * REACH)):
            there = (offset == far_end) & (entry >= 0)
            place = jnp.where(offset == far_end, used[i], place)
            used[i] = used[i] + there.astype(jnp.int32)
        code = jnp.where(entry >= 0, offset * slots + place, -1)
        bias = jnp.where(lane_code == code, 0.0, bias)
    out_ref[rows:, :] = bias.astype(jnp.bfloat16)


def pack_blocks(bank_ref, first_ref, second_ref, outs, slots):
    rows = bank_ref.shape[0] // 2
    block = rows // slots
    sector = lax.axis_index("lon")
    straight = side_of(1) == side_of(REACH)
    for (mine_ref, cross_ref), out in zip(((first_ref, second_ref), (second_ref, first_ref)), outs):
        picks = [jnp.int32(0)] * CAP
        used = jnp.int32(0)
        for e in range(first_ref.shape[0]):
            entry = jnp.where(straight, mine_ref[e], cross_ref[e])
            named = (entry >= 0) & (entry // slots == sector)
            for p in range(CAP):
                picks[p] = jnp.where(named & (used == p), entry % slots, picks[p])
            used = used + named.astype(jnp.int32)
        for half in range(2):
            for p in range(CAP):
                start = pl.multiple_of(half * rows + picks[p] * block, block)
                out[pl.ds((half * CAP + p) * block, block), :] = bank_ref[pl.ds(start, block), :]


def prep_pair(k_ref, v_ref, _after, out_ref):
    rows = out_ref.shape[0] // 2
    out_ref[:rows, :] = k_ref[...].reshape(rows, out_ref.shape[1])
    out_ref[rows:, :] = v_ref[...].reshape(rows, out_ref.shape[1])


def prep_bank(bank_ref, out_ref):
    out_ref[...] = bank_ref[...].reshape(out_ref.shape)


def prep_packs(bank_ref, first_ref, second_ref, _one, _two, a_out, b_out, *, slots):
    pack_blocks(bank_ref, first_ref, second_ref, (a_out, b_out), slots)


def softmax_part(scores, values):
    largest = jnp.max(scores, axis=1, keepdims=True)
    weights = jnp.exp2((scores - largest) * SCALE2)
    total = jnp.sum(weights, axis=1, keepdims=True)
    mixed = jnp.dot(weights.astype(jnp.bfloat16), values, preferred_element_type=jnp.float32)
    return mixed, jnp.maximum(largest * SCALE2, FLOOR), total


def near_part(queries, tiles, head):
    band = lax.axis_index("lat")
    bands = lax.axis_size("lat")
    rows = tiles[0].shape[0] // 2
    meets = (band % 2 == 1) & (band < bands - 1) | (band % 2 == 0) & (band > 0)
    shut = jnp.where(meets, 0.0, MASKED).astype(jnp.float32)
    scores = [dot_t(queries, tile[:rows, columns(head)]) for tile in tiles]
    scores[2] = scores[2] + shut
    values = [tile[rows:, columns(head)] for tile in tiles]
    return softmax_part(jnp.concatenate(scores, axis=1), jnp.concatenate(values, axis=0))


def far_part(queries, ref, bias, head):
    rows = ref.shape[0] // 2
    scores = dot_t(queries, ref[:rows, columns(head)]) + bias
    return softmax_part(scores, ref[rows:, columns(head)])


def mask_of(q_ref, offset, keys, stride):
    rows = q_ref.shape[0] - CODE_ROWS
    return q_ref[rows:, pl.ds((offset + REACH) * stride, keys)].astype(jnp.float32)[:1]


def mask_for(q_ref, index, distance, keys, stride):
    down, up = (mask_of(q_ref, x, keys, stride) for x in (-distance, distance))
    above = (side_of() > 0) if index == 0 else (side_of() < 0)
    return jnp.where(above, down, up)


def lanes_of(rows):
    return lax.broadcasted_iota(jnp.int32, (rows, STAT), 1)


def peak_of(mixed):
    return jnp.max(jnp.abs(mixed), axis=1, keepdims=True)


def power_of(peak):
    return jnp.ceil(jnp.log2(jnp.maximum(peak, 1e-30)))


def put_code(out_ref, values, head):
    out_ref[:, columns(head)] = ((values + ROUNDER) - ROUNDER).astype(jnp.int32).astype(jnp.int16)


def coded_stats(level, power, heads):
    live = lanes_of(level.shape[0]) < heads
    whole = jnp.floor(level)
    low = jnp.minimum(jnp.floor((level - whole) * 32768.0), 32767.0)
    whole, low, power = (jnp.where(live, x, 0.0) for x in (whole, low, power))
    return whole + pltpu.roll(low, LOW_LANE, 1) + pltpu.roll(power, EXP_LANE, 1)


def put_stats(out_ref, stats):
    out_ref[:, out_ref.shape[1] - STAT :] = stats.astype(jnp.int32).astype(jnp.int16)


def near_sides(a_ref, b_ref, own_ref, mate_ref, other_ref, _after, a_out, b_out, a_mix, b_mix):
    rows = a_out.shape[0]
    heads = own_ref.shape[1] // HEAD_DIM
    lanes = lanes_of(rows)
    sides = ((a_out, a_mix), (b_out, b_mix))
    tops, totals, peaks = ([jnp.ones((rows, STAT), jnp.float32) for _ in sides] for _ in range(3))
    for head in range(heads):
        queries = jnp.concatenate([a_ref[:rows, columns(head)], b_ref[:rows, columns(head)]], axis=0)
        mixed, top, total = near_part(queries, (own_ref, mate_ref, other_ref), head)
        peak = peak_of(mixed)
        for i, (_, mix) in enumerate(sides):
            cut = slice(i * rows, (i + 1) * rows)
            mix[:, columns(head)] = mixed[cut]
            tops[i] = jnp.where(lanes == head, top[cut], tops[i])
            totals[i] = jnp.where(lanes == head, total[cut], totals[i])
            peaks[i] = jnp.where(lanes == head, peak[cut], peaks[i])
    for (out, mix), top, total, peak in zip(sides, tops, totals, peaks):
        inverse = 1.0 / total
        power = power_of(peak * inverse)
        scale = inverse * jnp.exp2(14.0 - power)
        put_stats(out, coded_stats(jnp.maximum(top + jnp.log2(total), FLOOR), power, heads))
        for head in range(heads):
            put_code(out, mix[:, columns(head)] * scale[:, head : head + 1], head)


def far_sides(a_ref, b_ref, bank_ref, _after, a_mix, b_mix, a_stat, b_stat):
    rows = a_mix.shape[0]
    keys = bank_ref.shape[0] // 2
    lanes = lanes_of(rows)
    for index, (ref, mix, stat) in enumerate(((a_ref, a_mix, a_stat), (b_ref, b_mix, b_stat))):
        bias = mask_for(ref, index, 1, keys, keys)
        packed = [jnp.zeros((rows, STAT), jnp.float32) for _ in range(3)]
        for head in range(bank_ref.shape[1] // HEAD_DIM):
            mixed, top, total = far_part(ref[:rows, columns(head)], bank_ref, bias, head)
            mix[:, columns(head)] = mixed
            packed = [
                jnp.where(lanes == head, x, p) for x, p in zip((top, total, peak_of(mixed)), packed)
            ]
        for i, p in enumerate(packed):
            stat[:, i * STAT : (i + 1) * STAT] = p


def far_beyond(
    a_ref, b_ref, a_part, b_part, a_stat, b_stat, a_pack, b_pack, a_out, b_out, mix, *, keys
):
    rows, width = a_part.shape
    heads = width // HEAD_DIM
    packed = a_pack.shape[0] // 2
    masks = [mask_for(ref, index, 2, packed, keys) for index, ref in enumerate((a_ref, b_ref))]
    masks = [jnp.broadcast_to(mask, (rows, packed)) for mask in masks]
    closed = jnp.full((rows, packed), MASKED, jnp.float32)
    bias = jnp.concatenate(
        [jnp.concatenate([masks[0], closed], axis=1), jnp.concatenate([closed, masks[1]], axis=1)], axis=0
    )
    lanes = lanes_of(2 * rows)
    news = [jnp.zeros((2 * rows, STAT), jnp.float32) for _ in range(3)]
    for head in range(heads):
        cut = columns(head)
        queries = jnp.concatenate([a_ref[:rows, cut], b_ref[:rows, cut]], axis=0)
        far_keys = jnp.concatenate([b_pack[:packed, cut], a_pack[:packed, cut]], axis=0)
        far_values = jnp.concatenate([b_pack[packed:, cut], a_pack[packed:, cut]], axis=0)
        mixed, top, total = softmax_part(dot_t(queries, far_keys) + bias, far_values)
        mix[:, cut] = mixed
        news = [jnp.where(lanes == head, x, p) for x, p in zip((top, total, peak_of(mixed)), news)]
    lanes = lanes_of(rows)
    for index, (part, stat, out) in enumerate(((a_part, a_stat, a_out), (b_part, b_stat, b_out))):
        half = slice(index * rows, (index + 1) * rows)
        new = [x[half] for x in news]
        olds = [stat[:, i * STAT : (i + 1) * STAT] for i in range(3)]
        largest = jnp.maximum(olds[0], new[0])
        old_share, new_share = jnp.exp2(olds[0] - largest), jnp.exp2(new[0] - largest)
        total = jnp.where(lanes < heads, olds[1] * old_share + new[1] * new_share, 1.0)
        inverse = 1.0 / total
        old_share, new_share = old_share * inverse, new_share * inverse
        power = power_of(olds[2] * old_share + new[2] * new_share)
        scale = jnp.exp2(14.0 - power)
        old_share, new_share = old_share * scale, new_share * scale
        put_stats(out, coded_stats(jnp.maximum(largest + jnp.log2(total), FLOOR), power, heads))
        for head in range(heads):
            one, cut = slice(head, head + 1), columns(head)
            put_code(out, part[:, cut] * old_share[:, one] + mix[half, cut] * new_share[:, one], head)


def part_own(q_ref, own_ref, mate_ref, other_ref, bank_ref, near_out, far_out, stat_out):
    rows = near_out.shape[0]
    keys = bank_ref.shape[0] // 2
    lanes = lanes_of(rows)
    bias = mask_of(q_ref, 0, keys, keys)
    tops = jnp.full((rows, STAT), FLOOR, jnp.float32)
    totals = jnp.ones((rows, STAT), jnp.float32)
    for head in range(own_ref.shape[1] // HEAD_DIM):
        queries = q_ref[:rows, columns(head)]
        for mixed, top, total, out, lane in (
            near_part(queries, (own_ref, mate_ref, other_ref), head) + (near_out, head),
            far_part(queries, bank_ref, bias, head) + (far_out, FAR_LANE + head),
        ):
            out[:, columns(head)] = mixed
            tops = jnp.where(lanes == lane, top, tops)
            totals = jnp.where(lanes == lane, total, totals)
    stat_out[:, :STAT] = jnp.maximum(tops + jnp.log2(totals), FLOOR)
    stat_out[:, STAT:] = 1.0 / totals


def merge(near_ref, far_ref, own_ref, a_near, b_near, a_far, b_far, out_ref):
    width = near_ref.shape[1]
    sides = ((a_near, a_far), (b_near, b_far))
    levels, factors = [own_ref[:, :STAT]], [own_ref[:, STAT:]]
    for refs in sides:
        near, far = (ref[:, width:].astype(jnp.int32).astype(jnp.float32) for ref in refs)
        stat = near + pltpu.roll(far, FAR_LANE, 1)
        low = pltpu.roll(stat, STAT - LOW_LANE, 1)
        power = pltpu.roll(stat, STAT - EXP_LANE, 1)
        levels.append(stat + low * (1.0 / 32768.0))
        factors.append(jnp.exp2(power - 14.0))
    largest = functools.reduce(jnp.maximum, levels)
    weights = [jnp.exp2(level - largest) for level in levels]
    inverse = 1.0 / functools.reduce(jnp.add, weights)
    shares = [w * inverse * f for w, f in zip(weights, factors)]
    for head in range(width // HEAD_DIM):
        lanes = (slice(head, head + 1), slice(FAR_LANE + head, FAR_LANE + head + 1))
        total = sum(ref[:, columns(head)] * shares[0][:, lane] for ref, lane in zip((near_ref, far_ref), lanes))
        for refs, share in zip(sides, shares[1:]):
            for ref, lane in zip(refs, lanes):
                total += ref[:, columns(head)].astype(jnp.int32).astype(jnp.float32) * share[:, lane]
        out_ref[:, :, :, columns(head)] = total.astype(jnp.bfloat16).reshape(out_ref.shape[:3] + (HEAD_DIM,))


def swapped(value, first, axis="lon", reach=1, closed=True):
    count = lax.axis_size(axis)
    pairs = []
    for i in range(count):
        up = (i // reach) % 2 == first
        partner = i + reach if up else i - reach
        if closed or 0 <= partner < count:
            pairs.append((i, partner % count))
    return lax.ppermute(value, axis, pairs)


def side_of(reach=1):
    return 1 - 2 * ((lax.axis_index("lon") // reach) % 2)


def local(queries, token_keys, token_values, memory_bank, memory_ids, memory_count):
    frames, band_rows, tile_cols, width = queries.shape
    rows = frames * band_rows * tile_cols
    slots = memory_bank.shape[1]
    sectors = lax.axis_size("lon")
    shape = jax.ShapeDtypeStruct

    entries = memory_ids.reshape(-1)
    wanted = jnp.where(jnp.arange(entries.shape[0]) < memory_count.reshape(()), entries, -1)
    block = band_rows * tile_cols
    keys = slots * block
    bank = call(prep_bank, shape((2 * keys, width), jnp.bfloat16), [VMEM], memory_bank)
    packs = shape((2 * CAP * block, width), jnp.bfloat16)
    queries_shape = shape((rows + CODE_ROWS, width), jnp.bfloat16)
    first, second = swapped(wanted, 0, reach=REACH), swapped(wanted, 1, reach=REACH)
    coded_queries = call(
        functools.partial(prep_queries, slots=slots, sectors=sectors), queries_shape, [VMEM, SMEM], queries, wanted
    )
    q_b, q_a = swapped(coded_queries, 1), swapped(coded_queries, 0)
    pack_a, pack_b = call(
        functools.partial(prep_packs, slots=slots), [packs, packs], [VMEM, SMEM, SMEM, ANY, ANY],
        bank, first, second, q_a, q_b,
    )
    from_b, from_a = swapped(pack_b, 1), swapped(pack_a, 0)
    pair = call(
        prep_pair, shape((2 * rows, width), jnp.bfloat16), [VMEM, VMEM, ANY],
        token_keys, token_values, coded_queries,
    )
    other = swapped(pair, 1, "lat", closed=False)
    late = call(
        prep_pair, shape((2 * rows, width), jnp.bfloat16), [VMEM, VMEM, ANY],
        token_keys, token_values, first,
    )
    mate = swapped(late, 0, "lat", closed=False)
    plain = shape((rows, width), jnp.float32)
    work = pltpu.VMEM((rows, width), jnp.float32)
    near, far, own_stat = call(
        part_own, [plain, plain, shape((rows, 2 * STAT), jnp.float32)], [VMEM] * 5,
        coded_queries, pair, mate, other, bank,
    )
    coded = [shape((rows, width + STAT), jnp.int16)] * 2
    a_near, b_near = call(
        near_sides, coded, [VMEM] * 5 + [ANY], q_a, q_b, pair, mate, other, own_stat, scratch=[work, work]
    )
    back_b_near, back_a_near = swapped(b_near, 1), swapped(a_near, 0)
    stats = shape((rows, 3 * STAT), jnp.float32)
    a_far, b_far, a_stat, b_stat = call(
        far_sides, [plain, plain, stats, stats], [VMEM] * 3 + [ANY], q_a, q_b, bank, a_near
    )
    a_far, b_far = call(
        functools.partial(far_beyond, keys=keys), coded, [VMEM] * 8,
        q_a, q_b, a_far, b_far, a_stat, b_stat, from_a, from_b, scratch=[pltpu.VMEM((2 * rows, width), jnp.float32)],
    )
    back_b_far, back_a_far = swapped(b_far, 1), swapped(a_far, 0)
    return call(
        merge, shape(queries.shape, jnp.bfloat16), [VMEM] * 7,
        near, far, own_stat, back_a_near, back_b_near, back_a_far, back_b_far,
    )


def solution(mesh):
    placed = (
        P(None, "lat", "lon", None),
        P(None, "lat", "lon", None),
        P(None, "lat", "lon", None),
        P(None, None, "lat", "lon", None),
        P("lat", "lon", None),
        P("lat", "lon"),
    )
    return jax.shard_map(
        local, mesh=mesh, in_specs=placed, out_specs=P(None, "lat", "lon", None), check_vma=False
    )
```

time: 96.8 us -> 75.7 us (0.78)
  waiting for transfers between devices: 28.5 us -> 16.2 us
  starting transfers between devices: 40.6 us -> 35 us
  Pallas kernels: 22.9 us -> 19.8 us
    ppermute x10 -> x12, waiting for transfers between devices: 28.5 us -> 16.2 us  [swapped(): return lax.ppermute(value, axis, pairs)]
    ppermute x10 -> x12, starting transfers between devices: 40.6 us -> 35 us  [swapped(): return lax.ppermute(value, axis, pairs)]
    pallas_call x7 -> x10, Pallas kernels: 22.9 us -> 19.8 us  [call(): pl.pallas_call(body, out_shape=out_shape, in_specs=in_specs, out_specs=VM...]
    unnamed x14 -> x8, local copies, waits for them, and re-layouts: 3.87 us -> 2.99 us
  transfers between devices with their start and end apart: 10 -> 12, of which waited for: 2 -> 4; matrix products, arithmetic and copies ran while one was open for 0% -> 0% of each run, Pallas kernels for 21% -> 22%
where the time goes in v2:
time: 75.7 us; the launch traced here: 75.5 us
  starting transfers between devices  35 us (46%)
  Pallas kernels  19.8 us (26%)
  waiting for transfers between devices  16.2 us (21%)
  local copies, waits for them, and re-layouts  2.99 us (4%)
  between operations  0.78 us (1%)
    ppermute x12, starting transfers between devices, swapped(): return lax.ppermute(value, axis, pairs)  35 us
    pallas_call x10, Pallas kernels, call(): pl.pallas_call(body, out_shape=out_shape, in_specs=in_specs, out_specs=VM...  19.8 us
    ppermute x12, waiting for transfers between devices, swapped(): return lax.ppermute(value, axis, pairs)  16.2 us
    unnamed x8, local copies, waits for them, and re-layouts  2.99 us
  transfers between devices with their start and end apart: 12, of which 4 were waited for; matrix products, arithmetic and copies ran while one was open for 0% of the time, Pallas kernels for 22%

profile of v2, /device:TPU:1, one launch (start us, length us, event | category | flops | bytes accessed | tf_op | source)
XLA Modules:
  0.0 75.5 jit_solution(10851654081178346249)
XLA Ops:
  0.7 0.7 compare_select_fusion.ids_ref
  1.3 1.0 %copy-done.3 = bf16[4,16,2,1536]{3,2,1,0:T(2,128)(2,1)S(1)} copy-done((bf16[4,16,2,1536]{3,2,1,0:T(2,128)(2,1)S(1)}, bf16[4,16,2,1536]{3,2,1,0:T(2,128)(2,1)}, u32[]{:S(2)}) %copy-start.3) | copy-done | bytes 393240
  2.3 0.7 shard_map.64._after.q_ref
  3.0 2.6 %collective-permute-start.3 = (bf16[144,1536]{1,0:T(8,128)(2,1)S(1)}, bf16[144,1536]{1,0:T(8,128)(2,1)S(1)}, u32[]{:S(2)}, u32[]{:S(2)}) collective-permute-start(bf16[144,1536]{1,0:T(8,128)(2,1)S(1)} %shard_map.64._after.q_ref), channel_id=1, source_target_pairs={{0,4},{4,0},{8,12},{12,8},{16,20},{20,16},{24,28},{28,24},{32,36},... | collective-permute-start | bytes 1327112 | tf_op jit(solution)/shard_map/ppermute | solution.py:305
  5.6 9.6 %collective-permute-start.4 = (bf16[144,1536]{1,0:T(8,128)(2,1)S(1)}, bf16[144,1536]{1,0:T(8,128)(2,1)S(1)}, u32[]{:S(2)}, u32[]{:S(2)}) collective-permute-start(bf16[144,1536]{1,0:T(8,128)(2,1)S(1)} %shard_map.64._after.q_ref), channel_id=1, source_target_pairs={{0,252},{4,8},{8,4},{12,16},{16,12},{20,24},{24,20},{28,32},{32,28... | collective-permute-start | bytes 1327112 | tf_op jit(solution)/shard_map/ppermute | solution.py:305
  15.1 1.6 %collective-permute-start.7 = (s32[8]{0:T(128)S(1)}, s32[8]{0:T(128)S(1)}, u32[]{:S(2)}, u32[]{:S(2)}) collective-permute-start(s32[8]{0:T(128)S(1)} %compare_select_fusion.ids_ref), channel_id=1, source_target_pairs={{0,248},{4,252},{8,16},{12,20},{16,8},{20,12},{24,32},{28,36},{32,... | collective-permute-start | bytes 104 | tf_op jit(solution)/shard_map/ppermute | solution.py:305
  16.8 1.0 %copy-done.1 = bf16[4,16,2,1536]{3,2,1,0:T(2,128)(2,1)S(1)} copy-done((bf16[4,16,2,1536]{3,2,1,0:T(2,128)(2,1)S(1)}, bf16[4,16,2,1536]{3,2,1,0:T(2,128)(2,1)}, u32[]{:S(2)}) %copy-start.1) | copy-done | bytes 393240
  17.8 1.0 %copy-done.2 = bf16[4,16,2,1536]{3,2,1,0:T(2,128)(2,1)S(1)} copy-done((bf16[4,16,2,1536]{3,2,1,0:T(2,128)(2,1)S(1)}, bf16[4,16,2,1536]{3,2,1,0:T(2,128)(2,1)}, u32[]{:S(2)}) %copy-start.2) | copy-done | bytes 393240
  18.9 3.6 %collective-permute-start.2 = (bf16[256,1536]{1,0:T(8,128)(2,1)S(1)}, bf16[256,1536]{1,0:T(8,128)(2,1)S(1)}, u32[]{:S(2)}, u32[]{:S(2)}) collective-permute-start(bf16[256,1536]{1,0:T(8,128)(2,1)S(1)} %shard_map.65.own_ref), channel_id=1, source_target_pairs={{1,2},{2,1},{5,6},{6,5},{9,10},{10,9},{13,14},{14,13},{17,18},{18,... | collective-permute-start | bytes 2359304 | tf_op jit(solution)/shard_map/ppermute | solution.py:305
  22.9 2.0 %collective-permute-done.7.second_ref = s32[8]{0:T(128)S(1)} collective-permute-done((s32[8]{0:T(128)S(1)}, s32[8]{0:T(128)S(1)}, u32[]{:S(2)}, u32[]{:S(2)}) %collective-permute-start.7) | collective-permute-done | bytes 64 | tf_op jit(solution)/shard_map/ppermute | solution.py:305
  24.9 0.8 %shard_map.71 = (bf16[256,1536]{1,0:T(8,128)(2,1)S(1)}, bf16[256,1536]{1,0:T(8,128)(2,1)S(1)}) custom-call(bf16[512,1536]{1,0:T(8,128)(2,1)S(1)} %shard_map.67.bank_ref, s32[8]{0:T(128)S(1)} %collective-permute-done._after.first_ref, s32[8]{0:T(128)S(1)} %collective-permute-done.7.second_ref, bf16[144,1536]{1,0:T(8,128)(2,1)S(1)} %collective-permute-done.3.a_ref._one, ...), custom_call_target="tpu_custom_call" | custom-call | tf_op jit(solution)/shard_map/pallas_call | solution.py:31
  25.7 0.8 %collective-permute-start.8 = (bf16[256,1536]{1,0:T(8,128)(2,1)S(1)}, bf16[256,1536]{1,0:T(8,128)(2,1)S(1)}, u32[]{:S(2)}, u32[]{:S(2)}) collective-permute-start(bf16[256,1536]{1,0:T(8,128)(2,1)S(1)} %get-tuple-element.27), channel_id=1, source_target_pairs={{0,4},{4,0},{8,12},{12,8},{16,20},{20,16},{24,28},{28,24},{32,36},... | collective-permute-start | bytes 2359304 | tf_op jit(solution)/shard_map/ppermute | solution.py:305
  26.5 6.9 %collective-permute-start.9 = (bf16[256,1536]{1,0:T(8,128)(2,1)S(1)}, bf16[256,1536]{1,0:T(8,128)(2,1)S(1)}, u32[]{:S(2)}, u32[]{:S(2)}) collective-permute-start(bf16[256,1536]{1,0:T(8,128)(2,1)S(1)} %get-tuple-element.28), channel_id=1, source_target_pairs={{0,252},{4,8},{8,4},{12,16},{16,12},{20,24},{24,20},{28,32},{32,28... | collective-permute-start | bytes 2359304 | tf_op jit(solution)/shard_map/ppermute | solution.py:305
  33.4 6.1 %shard_map.68 = (f32[128,1536]{1,0:T(8,128)S(1)}, f32[128,1536]{1,0:T(8,128)S(1)}, f32[128,256]{1,0:T(8,128)S(1)}) custom-call(bf16[144,1536]{1,0:T(8,128)(2,1)S(1)} %shard_map.64._after.q_ref, bf16[256,1536]{1,0:T(8,128)(2,1)S(1)} %shard_map.65.own_ref, bf16[256,1536]{1,0:T(8,128)(2,1)S(1)} %collective-permute-done.1.mate_ref, ...), custom_call_target="tpu_custom_call" | custom-call | tf_op jit(solution)/shard_map/pallas_call | solution.py:31
  39.5 4.8 %shard_map.69 = (s16[128,1664]{1,0:T(8,128)(2,1)S(1)}, s16[128,1664]{1,0:T(8,128)(2,1)S(1)}) custom-call(bf16[144,1536]{1,0:T(8,128)(2,1)S(1)} %collective-permute-done.3.a_ref._one, bf16[144,1536]{1,0:T(8,128)(2,1)S(1)} %collective-permute-done.4.b_ref._two, bf16[256,1536]{1,0:T(8,128)(2,1)S(1)} %shard_map.65.own_ref, ...), custom_call_target="tpu_custom_call" | custom-call | tf_op jit(solution)/shard_map/pallas_call | solution.py:31
  44.3 0.8 %collective-permute-start.5 = (s16[128,1664]{1,0:T(8,128)(2,1)S(1)}, s16[128,1664]{1,0:T(8,128)(2,1)S(1)}, u32[]{:S(2)}, u32[]{:S(2)}) collective-permute-start(s16[128,1664]{1,0:T(8,128)(2,1)S(1)} %get-tuple-element.21._after), channel_id=1, source_target_pairs={{0,4},{4,0},{8,12},{12,8},{16,20},{20,16},{24,28},{28,24},{32,36},... | collective-permute-start | bytes 1277960 | tf_op jit(solution)/shard_map/ppermute | solution.py:305
  45.1 5.6 %collective-permute-start.6 = (s16[128,1664]{1,0:T(8,128)(2,1)S(1)}, s16[128,1664]{1,0:T(8,128)(2,1)S(1)}, u32[]{:S(2)}, u32[]{:S(2)}) collective-permute-start(s16[128,1664]{1,0:T(8,128)(2,1)S(1)} %get-tuple-element.22), channel_id=1, source_target_pairs={{0,252},{4,8},{8,4},{12,16},{16,12},{20,24},{24,20},{28,32},{32,28... | collective-permute-start | bytes 1277960 | tf_op jit(solution)/shard_map/ppermute | solution.py:305
  50.7 1.8 %shard_map.70 = (f32[128,1536]{1,0:T(8,128)S(1)}, f32[128,1536]{1,0:T(8,128)S(1)}, f32[128,384]{1,0:T(8,128)S(1)}, f32[128,384]{1,0:T(8,128)S(1)}) custom-call(bf16[144,1536]{1,0:T(8,128)(2,1)S(1)} %collective-permute-done.3.a_ref._one, bf16[144,1536]{1,0:T(8,128)(2,1)S(1)} %collective-permute-done.4.b_ref._two, bf16[512,1536]{1,0:T(8,128)(2,1)S(1)} %shard_map.67.bank_ref, ...), custom_call_target="tpu_custom_call" | custom-call | tf_op jit(solution)/shard_map/pallas_call | solution.py:31
  52.5 2.9 %shard_map.72 = (s16[128,1664]{1,0:T(8,128)(2,1)S(1)}, s16[128,1664]{1,0:T(8,128)(2,1)S(1)}) custom-call(bf16[144,1536]{1,0:T(8,128)(2,1)S(1)} %collective-permute-done.3.a_ref._one, bf16[144,1536]{1,0:T(8,128)(2,1)S(1)} %collective-permute-done.4.b_ref._two, f32[128,1536]{1,0:T(8,128)S(1)} %get-tuple-element.23.a_part, ...), custom_call_target="tpu_custom_call" | custom-call | tf_op jit(solution)/shard_map/pallas_call | solution.py:31
  55.5 3.3 %collective-permute-start.11 = (s16[128,1664]{1,0:T(8,128)(2,1)S(1)}, s16[128,1664]{1,0:T(8,128)(2,1)S(1)}, u32[]{:S(2)}, u32[]{:S(2)}) collective-permute-start(s16[128,1664]{1,0:T(8,128)(2,1)S(1)} %get-tuple-element.30), channel_id=1, source_target_pairs={{0,252},{4,8},{8,4},{12,16},{16,12},{20,24},{24,20},{28,32},{32,28... | collective-permute-start | bytes 1277960 | tf_op jit(solution)/shard_map/ppermute | solution.py:305
  58.9 1.1 %collective-permute-done.6.b_near = s16[128,1664]{1,0:T(8,128)(2,1)S(1)} collective-permute-done((s16[128,1664]{1,0:T(8,128)(2,1)S(1)}, s16[128,1664]{1,0:T(8,128)(2,1)S(1)}, u32[]{:S(2)}, u32[]{:S(2)}) %collective-permute-start.6) | collective-permute-done | bytes 426016 | tf_op jit(solution)/shard_map/ppermute | solution.py:305
  59.9 7.3 %collective-permute-done.10.a_far = s16[128,1664]{1,0:T(8,128)(2,1)S(1)} collective-permute-done((s16[128,1664]{1,0:T(8,128)(2,1)S(1)}, s16[128,1664]{1,0:T(8,128)(2,1)S(1)}, u32[]{:S(2)}, u32[]{:S(2)}) %collective-permute-start.10) | collective-permute-done | bytes 426016 | tf_op jit(solution)/shard_map/ppermute | solution.py:305
  67.2 5.8 %collective-permute-done.11.b_far = s16[128,1664]{1,0:T(8,128)(2,1)S(1)} collective-permute-done((s16[128,1664]{1,0:T(8,128)(2,1)S(1)}, s16[128,1664]{1,0:T(8,128)(2,1)S(1)}, u32[]{:S(2)}, u32[]{:S(2)}) %collective-permute-start.11) | collective-permute-done | bytes 426016 | tf_op jit(solution)/shard_map/ppermute | solution.py:305
  73.0 2.4 %shard_map.73 = bf16[4,16,2,1536]{3,2,1,0:T(2,128)(2,1)} custom-call(f32[128,1536]{1,0:T(8,128)S(1)} %get-tuple-element.18.near_ref, f32[128,1536]{1,0:T(8,128)S(1)} %get-tuple-element.19.far_ref, f32[128,256]{1,0:T(8,128)S(1)} %get-tuple-element.20._after.own_ref, s16[128,1664]{1,0:T(8,128)(2,1)S(1)} %collective-permute-done.5.a_near, ...), custom_call_target="tpu_custom_call" | custom-call | tf_op jit(solution)/shard_map/pallas_call | solution.py:31
  (19 shorter events, 0.6 us)
Async XLA Ops:
  1.3 1.0 %copy-start.3 = (bf16[4,16,2,1536]{3,2,1,0:T(2,128)(2,1)S(1)}, bf16[4,16,2,1536]{3,2,1,0:T(2,128)(2,1)}, u32[]{:S(2)}) copy-start(bf16[4,16,2,1536]{3,2,1,0:T(2,128)(2,1)} %q_ref.1) | copy-start | bytes 1179652
  3.0 19.7 %copy-start = (bf16[2,8,16,2,1536]{4,3,2,1,0:T(2,128)(2,1)S(1)}, bf16[2,8,16,2,1536]{4,3,2,1,0:T(2,128)(2,1)}, u32[]{:S(2)}) copy-start(bf16[2,8,16,2,1536]{4,3,2,1,0:T(2,128)(2,1)} %bank_ref.1) | copy-start | bytes 4718596
  3.0 21.9 %collective-permute-start.3 = (bf16[144,1536]{1,0:T(8,128)(2,1)S(1)}, bf16[144,1536]{1,0:T(8,128)(2,1)S(1)}, u32[]{:S(2)}, u32[]{:S(2)}) collective-permute-start(bf16[144,1536]{1,0:T(8,128)(2,1)S(1)} %shard_map.64._after.q_ref), channel_id=1, source_target_pairs={{0,4},{4,0},{8,12},{12,8},{16,20},{20,16},{24,28},{28,24},{32,36},... | collective-permute-start | bytes 1327112 | tf_op jit(solution)/shard_map/ppermute | solution.py:305
  5.6 19.3 %collective-permute-start.4 = (bf16[144,1536]{1,0:T(8,128)(2,1)S(1)}, bf16[144,1536]{1,0:T(8,128)(2,1)S(1)}, u32[]{:S(2)}, u32[]{:S(2)}) collective-permute-start(bf16[144,1536]{1,0:T(8,128)(2,1)S(1)} %shard_map.64._after.q_ref), channel_id=1, source_target_pairs={{0,252},{4,8},{8,4},{12,16},{16,12},{20,24},{24,20},{28,32},{32,28... | collective-permute-start | bytes 1327112 | tf_op jit(solution)/shard_map/ppermute | solution.py:305
  15.1 7.3 %collective-permute-start = (s32[8]{0:T(128)S(1)}, s32[8]{0:T(128)S(1)}, u32[]{:S(2)}, u32[]{:S(2)}) collective-permute-start(s32[8]{0:T(128)S(1)} %compare_select_fusion.ids_ref), channel_id=1, source_target_pairs={{0,8},{4,12},{8,0},{12,4},{16,24},{20,28},{24,16},{28,20},{32,40},... | collective-permute-start | bytes 104 | tf_op jit(solution)/shard_map/ppermute | solution.py:305
  15.1 9.8 %collective-permute-start.7 = (s32[8]{0:T(128)S(1)}, s32[8]{0:T(128)S(1)}, u32[]{:S(2)}, u32[]{:S(2)}) collective-permute-start(s32[8]{0:T(128)S(1)} %compare_select_fusion.ids_ref), channel_id=1, source_target_pairs={{0,248},{4,252},{8,16},{12,20},{16,8},{20,12},{24,32},{28,36},{32,... | collective-permute-start | bytes 104 | tf_op jit(solution)/shard_map/ppermute | solution.py:305
  16.8 1.0 %copy-start.1 = (bf16[4,16,2,1536]{3,2,1,0:T(2,128)(2,1)S(1)}, bf16[4,16,2,1536]{3,2,1,0:T(2,128)(2,1)}, u32[]{:S(2)}) copy-start(bf16[4,16,2,1536]{3,2,1,0:T(2,128)(2,1)} %k_ref.3) | copy-start | bytes 1179652
  17.8 1.0 %copy-start.2 = (bf16[4,16,2,1536]{3,2,1,0:T(2,128)(2,1)S(1)}, bf16[4,16,2,1536]{3,2,1,0:T(2,128)(2,1)}, u32[]{:S(2)}) copy-start(bf16[4,16,2,1536]{3,2,1,0:T(2,128)(2,1)} %v_ref.3) | copy-start | bytes 1179652
  18.9 14.6 %collective-permute-start.2 = (bf16[256,1536]{1,0:T(8,128)(2,1)S(1)}, bf16[256,1536]{1,0:T(8,128)(2,1)S(1)}, u32[]{:S(2)}, u32[]{:S(2)}) collective-permute-start(bf16[256,1536]{1,0:T(8,128)(2,1)S(1)} %shard_map.65.own_ref), channel_id=1, source_target_pairs={{1,2},{2,1},{5,6},{6,5},{9,10},{10,9},{13,14},{14,13},{17,18},{18,... | collective-permute-start | bytes 2359304 | tf_op jit(solution)/shard_map/ppermute | solution.py:305
  22.6 10.9 %collective-permute-start.1 = (bf16[256,1536]{1,0:T(8,128)(2,1)S(1)}, bf16[256,1536]{1,0:T(8,128)(2,1)S(1)}, u32[]{:S(2)}, u32[]{:S(2)}) collective-permute-start(bf16[256,1536]{1,0:T(8,128)(2,1)S(1)} %shard_map.66), channel_id=1, source_target_pairs={{0,1},{1,0},{2,3},{3,2},{4,5},{5,4},{6,7},{7,6},{8,9},{9,8},{10,11... | collective-permute-start | bytes 2359304 | tf_op jit(solution)/shard_map/ppermute | solution.py:305
  25.7 26.8 %collective-permute-start.8 = (bf16[256,1536]{1,0:T(8,128)(2,1)S(1)}, bf16[256,1536]{1,0:T(8,128)(2,1)S(1)}, u32[]{:S(2)}, u32[]{:S(2)}) collective-permute-start(bf16[256,1536]{1,0:T(8,128)(2,1)S(1)} %get-tuple-element.27), channel_id=1, source_target_pairs={{0,4},{4,0},{8,12},{12,8},{16,20},{20,16},{24,28},{28,24},{32,36},... | collective-permute-start | bytes 2359304 | tf_op jit(solution)/shard_map/ppermute | solution.py:305
  26.5 26.0 %collective-permute-start.9 = (bf16[256,1536]{1,0:T(8,128)(2,1)S(1)}, bf16[256,1536]{1,0:T(8,128)(2,1)S(1)}, u32[]{:S(2)}, u32[]{:S(2)}) collective-permute-start(bf16[256,1536]{1,0:T(8,128)(2,1)S(1)} %get-tuple-element.28), channel_id=1, source_target_pairs={{0,252},{4,8},{8,4},{12,16},{16,12},{20,24},{24,20},{28,32},{32,28... | collective-permute-start | bytes 2359304 | tf_op jit(solution)/shard_map/ppermute | solution.py:305
  44.3 14.6 %collective-permute-start.5 = (s16[128,1664]{1,0:T(8,128)(2,1)S(1)}, s16[128,1664]{1,0:T(8,128)(2,1)S(1)}, u32[]{:S(2)}, u32[]{:S(2)}) collective-permute-start(s16[128,1664]{1,0:T(8,128)(2,1)S(1)} %get-tuple-element.21._after), channel_id=1, source_target_pairs={{0,4},{4,0},{8,12},{12,8},{16,20},{20,16},{24,28},{28,24},{32,36},... | collective-permute-start | bytes 1277960 | tf_op jit(solution)/shard_map/ppermute | solution.py:305
  45.1 14.8 %collective-permute-start.6 = (s16[128,1664]{1,0:T(8,128)(2,1)S(1)}, s16[128,1664]{1,0:T(8,128)(2,1)S(1)}, u32[]{:S(2)}, u32[]{:S(2)}) collective-permute-start(s16[128,1664]{1,0:T(8,128)(2,1)S(1)} %get-tuple-element.22), channel_id=1, source_target_pairs={{0,252},{4,8},{8,4},{12,16},{16,12},{20,24},{24,20},{28,32},{32,28... | collective-permute-start | bytes 1277960 | tf_op jit(solution)/shard_map/ppermute | solution.py:305
  55.4 11.8 %collective-permute-start.10 = (s16[128,1664]{1,0:T(8,128)(2,1)S(1)}, s16[128,1664]{1,0:T(8,128)(2,1)S(1)}, u32[]{:S(2)}, u32[]{:S(2)}) collective-permute-start(s16[128,1664]{1,0:T(8,128)(2,1)S(1)} %get-tuple-element.29), channel_id=1, source_target_pairs={{0,4},{4,0},{8,12},{12,8},{16,20},{20,16},{24,28},{28,24},{32,36},... | collective-permute-start | bytes 1277960 | tf_op jit(solution)/shard_map/ppermute | solution.py:305
  55.5 17.5 %collective-permute-start.11 = (s16[128,1664]{1,0:T(8,128)(2,1)S(1)}, s16[128,1664]{1,0:T(8,128)(2,1)S(1)}, u32[]{:S(2)}, u32[]{:S(2)}) collective-permute-start(s16[128,1664]{1,0:T(8,128)(2,1)S(1)} %get-tuple-element.30), channel_id=1, source_target_pairs={{0,252},{4,8},{8,4},{12,16},{16,12},{20,24},{24,20},{28,32},{32,28... | collective-permute-start | bytes 1277960 | tf_op jit(solution)/shard_map/ppermute | solution.py:305

commit v3 on v2

--- a/solution.py
+++ b/solution.py
@@ -210,7 +210,7 @@
 
 
 def far_beyond(
-    a_ref, b_ref, a_part, b_part, a_stat, b_stat, a_pack, b_pack, a_out, b_out, mix, *, keys
+    a_ref, b_ref, a_part, b_part, a_stat, b_stat, a_pack, b_pack, _after, a_out, b_out, mix, *, keys
 ):
     rows, width = a_part.shape
     heads = width // HEAD_DIM
@@ -250,7 +250,7 @@
             put_code(out, part[:, cut] * old_share[:, one] + mix[half, cut] * new_share[:, one], head)
 
 
-def part_own(q_ref, own_ref, mate_ref, other_ref, bank_ref, near_out, far_out, stat_out):
+def part_own(q_ref, own_ref, mate_ref, other_ref, bank_ref, _after, near_out, far_out, stat_out):
     rows = near_out.shape[0]
     keys = bank_ref.shape[0] // 2
     lanes = lanes_of(rows)
@@ -270,13 +270,10 @@
     stat_out[:, STAT:] = 1.0 / totals
 
 
-def merge(near_ref, far_ref, own_ref, a_near, b_near, a_far, b_far, out_ref):
-    width = near_ref.shape[1]
-    sides = ((a_near, a_far), (b_near, b_far))
-    levels, factors = [own_ref[:, :STAT]], [own_ref[:, STAT:]]
-    for refs in sides:
-        near, far = (ref[:, width:].astype(jnp.int32).astype(jnp.float32) for ref in refs)
-        stat = near + pltpu.roll(far, FAR_LANE, 1)
+def shares_of(own_level, own_inverse, refs):
+    levels, factors = [own_level], [own_inverse]
+    for ref in refs:
+        stat = ref[:, ref.shape[1] - STAT :].astype(jnp.int32).astype(jnp.float32)
         low = pltpu.roll(stat, STAT - LOW_LANE, 1)
         power = pltpu.roll(stat, STAT - EXP_LANE, 1)
         levels.append(stat + low * (1.0 / 32768.0))
@@ -284,13 +281,28 @@
     largest = functools.reduce(jnp.maximum, levels)
     weights = [jnp.exp2(level - largest) for level in levels]
     inverse = 1.0 / functools.reduce(jnp.add, weights)
-    shares = [w * inverse * f for w, f in zip(weights, factors)]
-    for head in range(width // HEAD_DIM):
-        lanes = (slice(head, head + 1), slice(FAR_LANE + head, FAR_LANE + head + 1))
-        total = sum(ref[:, columns(head)] * shares[0][:, lane] for ref, lane in zip((near_ref, far_ref), lanes))
-        for refs, share in zip(sides, shares[1:]):
-            for ref, lane in zip(refs, lanes):
-                total += ref[:, columns(head)].astype(jnp.int32).astype(jnp.float32) * share[:, lane]
+    return [w * inverse * f for w, f in zip(weights, factors)]
+
+
+def mixed_by(shares, own_ref, refs, head):
+    one, cut = slice(head, head + 1), columns(head)
+    total = own_ref[:, cut] * shares[0][:, one]
+    for ref, share in zip(refs, shares[1:]):
+        total += ref[:, cut].astype(jnp.int32).astype(jnp.float32) * share[:, one]
+    return total
+
+
+def merge_near(own_ref, stat_ref, a_ref, b_ref, out_ref):
+    shares = shares_of(stat_ref[:, :STAT], stat_ref[:, STAT:], (a_ref, b_ref))
+    for head in range(own_ref.shape[1] // HEAD_DIM):
+        out_ref[:, columns(head)] = mixed_by(shares, own_ref, (a_ref, b_ref), head)
+
+
+def merge_far(near_ref, own_ref, stat_ref, a_ref, b_ref, out_ref):
+    own = [pltpu.roll(stat_ref[:, i * STAT : (i + 1) * STAT], STAT - FAR_LANE, 1) for i in range(2)]
+    shares = shares_of(*own, (a_ref, b_ref))
+    for head in range(own_ref.shape[1] // HEAD_DIM):
+        total = near_ref[:, columns(head)] + mixed_by(shares, own_ref, (a_ref, b_ref), head)
         out_ref[:, :, :, columns(head)] = total.astype(jnp.bfloat16).reshape(out_ref.shape[:3] + (HEAD_DIM,))
 
 
@@ -329,8 +341,7 @@
     )
     q_b, q_a = swapped(coded_queries, 1), swapped(coded_queries, 0)
     pack_a, pack_b = call(
-        functools.partial(prep_packs, slots=slots), [packs, packs], [VMEM, SMEM, SMEM, ANY, ANY],
-        bank, first, second, q_a, q_b,
+        functools.partial(prep_packs, slots=slots), [packs, packs], [VMEM, SMEM, SMEM, ANY, ANY], bank, first, second, q_a, q_b
     )
     from_b, from_a = swapped(pack_b, 1), swapped(pack_a, 0)
     pair = call(
@@ -345,27 +356,28 @@
     mate = swapped(late, 0, "lat", closed=False)
     plain = shape((rows, width), jnp.float32)
     work = pltpu.VMEM((rows, width), jnp.float32)
+    coded = [shape((rows, width + STAT), jnp.int16)] * 2
+    stats = shape((rows, 3 * STAT), jnp.float32)
+    a_part, b_part, a_stat, b_stat = call(
+        far_sides, [plain, plain, stats, stats], [VMEM] * 3 + [ANY], q_a, q_b, bank, coded_queries
+    )
+    a_near, b_near = call(
+        near_sides, coded, [VMEM] * 5 + [ANY], q_a, q_b, pair, mate, other, a_stat, scratch=[work, work]
+    )
+    back_b_near, back_a_near = swapped(b_near, 1), swapped(a_near, 0)
     near, far, own_stat = call(
-        part_own, [plain, plain, shape((rows, 2 * STAT), jnp.float32)], [VMEM] * 5,
-        coded_queries, pair, mate, other, bank,
-    )
-    coded = [shape((rows, width + STAT), jnp.int16)] * 2
-    a_near, b_near = call(
-        near_sides, coded, [VMEM] * 5 + [ANY], q_a, q_b, pair, mate, other, own_stat, scratch=[work, work]
-    )
-    back_b_near, back_a_near = swapped(b_near, 1), swapped(a_near, 0)
-    stats = shape((rows, 3 * STAT), jnp.float32)
-    a_far, b_far, a_stat, b_stat = call(
-        far_sides, [plain, plain, stats, stats], [VMEM] * 3 + [ANY], q_a, q_b, bank, a_near
+        part_own, [plain, plain, shape((rows, 2 * STAT), jnp.float32)], [VMEM] * 5 + [ANY],
+        coded_queries, pair, mate, other, bank, a_near,
     )
     a_far, b_far = call(
-        functools.partial(far_beyond, keys=keys), coded, [VMEM] * 8,
-        q_a, q_b, a_far, b_far, a_stat, b_stat, from_a, from_b, scratch=[pltpu.VMEM((2 * rows, width), jnp.float32)],
+        functools.partial(far_beyond, keys=keys), coded, [VMEM] * 8 + [ANY],
+        q_a, q_b, a_part, b_part, a_stat, b_stat, from_a, from_b, own_stat,
+        scratch=[pltpu.VMEM((2 * rows, width), jnp.float32)],
     )
     back_b_far, back_a_far = swapped(b_far, 1), swapped(a_far, 0)
+    near = call(merge_near, plain, [VMEM] * 4, near, own_stat, back_a_near, back_b_near)
     return call(
-        merge, shape(queries.shape, jnp.bfloat16), [VMEM] * 7,
-        near, far, own_stat, back_a_near, back_b_near, back_a_far, back_b_far,
+        merge_far, shape(queries.shape, jnp.bfloat16), [VMEM] * 5, near, far, own_stat, back_a_far, back_b_far
     )
 
 

time: 75.7 us -> 71.9 us (0.950)
  waiting for transfers between devices: 16.2 us -> 12 us
  Pallas kernels: 19.8 us -> 21.3 us
  starting transfers between devices: 35 us -> 33.6 us
    ppermute x12, waiting for transfers between devices: 16.2 us -> 12 us  [swapped(): return lax.ppermute(value, axis, pairs)]
    pallas_call x10 -> x11, Pallas kernels: 19.8 us -> 21.3 us  [call(): pl.pallas_call(body, out_shape=out_shape, in_specs=in_specs, out_specs=VM...]
    ppermute x12, starting transfers between devices: 35 us -> 33.6 us  [swapped(): return lax.ppermute(value, axis, pairs)]
    unnamed x8 -> x10, local copies, waits for them, and re-layouts: 2.99 us -> 3 us
  transfers between devices with their start and end apart: 12 -> 12, of which waited for: 4 -> 3; matrix products, arithmetic and copies ran while one was open for 0% -> 0% of each run, Pallas kernels for 22% -> 27%
where the time goes in v3:
time: 71.9 us; the launch traced here: 71.3 us
  starting transfers between devices  33.6 us (47%)
  Pallas kernels  21.3 us (30%)
  waiting for transfers between devices  12 us (17%)
  local copies, waits for them, and re-layouts  3 us (4%)
  between operations  0.83 us (1%)
    ppermute x12, starting transfers between devices, swapped(): return lax.ppermute(value, axis, pairs)  33.6 us
    pallas_call x11, Pallas kernels, call(): pl.pallas_call(body, out_shape=out_shape, in_specs=in_specs, out_specs=VM...  21.3 us
    ppermute x12, waiting for transfers between devices, swapped(): return lax.ppermute(value, axis, pairs)  12 us
    unnamed x10, local copies, waits for them, and re-layouts  3 us
  transfers between devices with their start and end apart: 12, of which 3 were waited for; matrix products, arithmetic and copies ran while one was open for 0% of the time, Pallas kernels for 27%

profile of v3, /device:TPU:1, one launch (start us, length us, event | category | flops | bytes accessed | tf_op | source)
XLA Modules:
  0.0 71.3 jit_solution(3344014280574088030)
XLA Ops:
  0.7 0.7 compare_select_fusion.ids_ref
  1.3 1.0 %copy-done.4 = bf16[4,16,2,1536]{3,2,1,0:T(2,128)(2,1)S(1)} copy-done((bf16[4,16,2,1536]{3,2,1,0:T(2,128)(2,1)S(1)}, bf16[4,16,2,1536]{3,2,1,0:T(2,128)(2,1)}, u32[]{:S(2)}) %copy-start.4) | copy-done | bytes 393240
  2.3 0.7 shard_map.64._after.q_ref
  3.0 2.6 %collective-permute-start.3 = (bf16[144,1536]{1,0:T(8,128)(2,1)S(1)}, bf16[144,1536]{1,0:T(8,128)(2,1)S(1)}, u32[]{:S(2)}, u32[]{:S(2)}) collective-permute-start(bf16[144,1536]{1,0:T(8,128)(2,1)S(1)} %shard_map.64._after.q_ref), channel_id=1, source_target_pairs={{0,4},{4,0},{8,12},{12,8},{16,20},{20,16},{24,28},{28,24},{32,36},... | collective-permute-start | bytes 1327112 | tf_op jit(solution)/shard_map/ppermute | solution.py:317
  5.6 9.6 %collective-permute-start.4 = (bf16[144,1536]{1,0:T(8,128)(2,1)S(1)}, bf16[144,1536]{1,0:T(8,128)(2,1)S(1)}, u32[]{:S(2)}, u32[]{:S(2)}) collective-permute-start(bf16[144,1536]{1,0:T(8,128)(2,1)S(1)} %shard_map.64._after.q_ref), channel_id=1, source_target_pairs={{0,252},{4,8},{8,4},{12,16},{16,12},{20,24},{24,20},{28,32},{32,28... | collective-permute-start | bytes 1327112 | tf_op jit(solution)/shard_map/ppermute | solution.py:317
  15.1 1.6 %collective-permute-start.7 = (s32[8]{0:T(128)S(1)}, s32[8]{0:T(128)S(1)}, u32[]{:S(2)}, u32[]{:S(2)}) collective-permute-start(s32[8]{0:T(128)S(1)} %compare_select_fusion.ids_ref), channel_id=1, source_target_pairs={{0,248},{4,252},{8,16},{12,20},{16,8},{20,12},{24,32},{28,36},{32,... | collective-permute-start | bytes 104 | tf_op jit(solution)/shard_map/ppermute | solution.py:317
  16.8 1.0 %copy-done.2 = bf16[4,16,2,1536]{3,2,1,0:T(2,128)(2,1)S(1)} copy-done((bf16[4,16,2,1536]{3,2,1,0:T(2,128)(2,1)S(1)}, bf16[4,16,2,1536]{3,2,1,0:T(2,128)(2,1)}, u32[]{:S(2)}) %copy-start.2) | copy-done | bytes 393240
  17.8 1.0 %copy-done.3 = bf16[4,16,2,1536]{3,2,1,0:T(2,128)(2,1)S(1)} copy-done((bf16[4,16,2,1536]{3,2,1,0:T(2,128)(2,1)S(1)}, bf16[4,16,2,1536]{3,2,1,0:T(2,128)(2,1)}, u32[]{:S(2)}) %copy-start.3) | copy-done | bytes 393240
  18.9 3.6 %collective-permute-start.2 = (bf16[256,1536]{1,0:T(8,128)(2,1)S(1)}, bf16[256,1536]{1,0:T(8,128)(2,1)S(1)}, u32[]{:S(2)}, u32[]{:S(2)}) collective-permute-start(bf16[256,1536]{1,0:T(8,128)(2,1)S(1)} %shard_map.65.own_ref), channel_id=1, source_target_pairs={{1,2},{2,1},{5,6},{6,5},{9,10},{10,9},{13,14},{14,13},{17,18},{18,... | collective-permute-start | bytes 2359304 | tf_op jit(solution)/shard_map/ppermute | solution.py:317
  22.7 0.2 shard_map.67.bank_ref
  22.9 2.0 %collective-permute-done.7.second_ref = s32[8]{0:T(128)S(1)} collective-permute-done((s32[8]{0:T(128)S(1)}, s32[8]{0:T(128)S(1)}, u32[]{:S(2)}, u32[]{:S(2)}) %collective-permute-start.7) | collective-permute-done | bytes 64 | tf_op jit(solution)/shard_map/ppermute | solution.py:317
  24.9 0.8 %shard_map.72 = (bf16[256,1536]{1,0:T(8,128)(2,1)S(1)}, bf16[256,1536]{1,0:T(8,128)(2,1)S(1)}) custom-call(bf16[512,1536]{1,0:T(8,128)(2,1)S(1)} %shard_map.67.bank_ref, s32[8]{0:T(128)S(1)} %collective-permute-done._after.first_ref, s32[8]{0:T(128)S(1)} %collective-permute-done.7.second_ref, bf16[144,1536]{1,0:T(8,128)(2,1)S(1)} %collective-permute-done.3.a_ref._one, ...), custom_call_target="tpu_custom_call" | custom-call | tf_op jit(solution)/shard_map/pallas_call | solution.py:31
  25.7 0.8 %collective-permute-start.8 = (bf16[256,1536]{1,0:T(8,128)(2,1)S(1)}, bf16[256,1536]{1,0:T(8,128)(2,1)S(1)}, u32[]{:S(2)}, u32[]{:S(2)}) collective-permute-start(bf16[256,1536]{1,0:T(8,128)(2,1)S(1)} %get-tuple-element.27), channel_id=1, source_target_pairs={{0,4},{4,0},{8,12},{12,8},{16,20},{20,16},{24,28},{28,24},{32,36},... | collective-permute-start | bytes 2359304 | tf_op jit(solution)/shard_map/ppermute | solution.py:317
  26.5 6.9 %collective-permute-start.9 = (bf16[256,1536]{1,0:T(8,128)(2,1)S(1)}, bf16[256,1536]{1,0:T(8,128)(2,1)S(1)}, u32[]{:S(2)}, u32[]{:S(2)}) collective-permute-start(bf16[256,1536]{1,0:T(8,128)(2,1)S(1)} %get-tuple-element.28), channel_id=1, source_target_pairs={{0,252},{4,8},{8,4},{12,16},{16,12},{20,24},{24,20},{28,32},{32,28... | collective-permute-start | bytes 2359304 | tf_op jit(solution)/shard_map/ppermute | solution.py:317
  33.4 1.8 %shard_map.68 = (f32[128,1536]{1,0:T(8,128)S(1)}, f32[128,1536]{1,0:T(8,128)S(1)}, f32[128,384]{1,0:T(8,128)S(1)}, f32[128,384]{1,0:T(8,128)S(1)}) custom-call(bf16[144,1536]{1,0:T(8,128)(2,1)S(1)} %collective-permute-done.3.a_ref._one, bf16[144,1536]{1,0:T(8,128)(2,1)S(1)} %collective-permute-done.4.b_ref._two, bf16[512,1536]{1,0:T(8,128)(2,1)S(1)} %shard_map.67.bank_ref, ...), custom_call_target="tpu_custom_call" | custom-call | tf_op jit(solution)/shard_map/pallas_call | solution.py:31
  35.2 4.8 %shard_map.69 = (s16[128,1664]{1,0:T(8,128)(2,1)S(1)}, s16[128,1664]{1,0:T(8,128)(2,1)S(1)}) custom-call(bf16[144,1536]{1,0:T(8,128)(2,1)S(1)} %collective-permute-done.3.a_ref._one, bf16[144,1536]{1,0:T(8,128)(2,1)S(1)} %collective-permute-done.4.b_ref._two, bf16[256,1536]{1,0:T(8,128)(2,1)S(1)} %shard_map.65.own_ref, ...), custom_call_target="tpu_custom_call" | custom-call | tf_op jit(solution)/shard_map/pallas_call | solution.py:31
  40.1 4.5 %collective-permute-start.6 = (s16[128,1664]{1,0:T(8,128)(2,1)S(1)}, s16[128,1664]{1,0:T(8,128)(2,1)S(1)}, u32[]{:S(2)}, u32[]{:S(2)}) collective-permute-start(s16[128,1664]{1,0:T(8,128)(2,1)S(1)} %get-tuple-element.22), channel_id=1, source_target_pairs={{0,252},{4,8},{8,4},{12,16},{16,12},{20,24},{24,20},{28,32},{32,28... | collective-permute-start | bytes 1277960 | tf_op jit(solution)/shard_map/ppermute | solution.py:317
  44.6 7.5 %shard_map.70 = (f32[128,1536]{1,0:T(8,128)S(1)}, f32[128,1536]{1,0:T(8,128)S(1)}, f32[128,256]{1,0:T(8,128)S(1)}) custom-call(bf16[144,1536]{1,0:T(8,128)(2,1)S(1)} %shard_map.64._after.q_ref, bf16[256,1536]{1,0:T(8,128)(2,1)S(1)} %shard_map.65.own_ref, bf16[256,1536]{1,0:T(8,128)(2,1)S(1)} %collective-permute-done.1.mate_ref, ...), custom_call_target="tpu_custom_call" | custom-call | tf_op jit(solution)/shard_map/pallas_call | solution.py:31
  52.2 2.9 %shard_map.73 = (s16[128,1664]{1,0:T(8,128)(2,1)S(1)}, s16[128,1664]{1,0:T(8,128)(2,1)S(1)}) custom-call(bf16[144,1536]{1,0:T(8,128)(2,1)S(1)} %collective-permute-done.3.a_ref._one, bf16[144,1536]{1,0:T(8,128)(2,1)S(1)} %collective-permute-done.4.b_ref._two, f32[128,1536]{1,0:T(8,128)S(1)} %get-tuple-element.24.a_part, ...), custom_call_target="tpu_custom_call" | custom-call | tf_op jit(solution)/shard_map/pallas_call | solution.py:31
  55.2 3.7 %collective-permute-start.11 = (s16[128,1664]{1,0:T(8,128)(2,1)S(1)}, s16[128,1664]{1,0:T(8,128)(2,1)S(1)}, u32[]{:S(2)}, u32[]{:S(2)}) collective-permute-start(s16[128,1664]{1,0:T(8,128)(2,1)S(1)} %get-tuple-element.30), channel_id=1, source_target_pairs={{0,252},{4,8},{8,4},{12,16},{16,12},{20,24},{24,20},{28,32},{32,28... | collective-permute-start | bytes 1277960 | tf_op jit(solution)/shard_map/ppermute | solution.py:317
  58.9 0.8 %shard_map.71.near_ref = f32[128,1536]{1,0:T(8,128)S(1)} custom-call(f32[128,1536]{1,0:T(8,128)S(1)} %get-tuple-element.20.own_ref, f32[128,256]{1,0:T(8,128)S(1)} %get-tuple-element.21.stat_ref._after, s16[128,1664]{1,0:T(8,128)(2,1)S(1)} %collective-permute-done.5.a_ref, s16[128,1664]{1,0:T(8,128)(2,1)S(1)} %collective-permute-done.6.b_ref), custom_call_target="tpu_custom_call" | custom-call | tf_op jit(solution)/shard_map/pallas_call | solution.py:31
  59.7 4.1 %collective-permute-done.10.a_ref = s16[128,1664]{1,0:T(8,128)(2,1)S(1)} collective-permute-done((s16[128,1664]{1,0:T(8,128)(2,1)S(1)}, s16[128,1664]{1,0:T(8,128)(2,1)S(1)}, u32[]{:S(2)}, u32[]{:S(2)}) %collective-permute-start.10) | collective-permute-done | bytes 426016 | tf_op jit(solution)/shard_map/ppermute | solution.py:317
  63.8 5.8 %collective-permute-done.11.b_ref = s16[128,1664]{1,0:T(8,128)(2,1)S(1)} collective-permute-done((s16[128,1664]{1,0:T(8,128)(2,1)S(1)}, s16[128,1664]{1,0:T(8,128)(2,1)S(1)}, u32[]{:S(2)}, u32[]{:S(2)}) %collective-permute-start.11) | collective-permute-done | bytes 426016 | tf_op jit(solution)/shard_map/ppermute | solution.py:317
  69.6 1.7 %shard_map.74 = bf16[4,16,2,1536]{3,2,1,0:T(2,128)(2,1)} custom-call(f32[128,1536]{1,0:T(8,128)S(1)} %shard_map.71.near_ref, f32[128,1536]{1,0:T(8,128)S(1)} %get-tuple-element.23.own_ref, f32[128,256]{1,0:T(8,128)S(1)} %get-tuple-element.21.stat_ref._after, s16[128,1664]{1,0:T(8,128)(2,1)S(1)} %collective-permute-done.10.a_ref, ...), custom_call_target="tpu_custom_call" | custom-call | tf_op jit(solution)/shard_map/pallas_call | solution.py:31
  (22 shorter events, 0.5 us)
Async XLA Ops:
  1.3 1.0 %copy-start.4 = (bf16[4,16,2,1536]{3,2,1,0:T(2,128)(2,1)S(1)}, bf16[4,16,2,1536]{3,2,1,0:T(2,128)(2,1)}, u32[]{:S(2)}) copy-start(bf16[4,16,2,1536]{3,2,1,0:T(2,128)(2,1)} %q_ref.1) | copy-start | bytes 1179652
  3.0 19.7 %copy-start.1 = (bf16[2,8,16,2,1536]{4,3,2,1,0:T(2,128)(2,1)S(1)}, bf16[2,8,16,2,1536]{4,3,2,1,0:T(2,128)(2,1)}, u32[]{:S(2)}) copy-start(bf16[2,8,16,2,1536]{4,3,2,1,0:T(2,128)(2,1)} %bank_ref.1) | copy-start | bytes 4718596
  3.0 21.9 %collective-permute-start.3 = (bf16[144,1536]{1,0:T(8,128)(2,1)S(1)}, bf16[144,1536]{1,0:T(8,128)(2,1)S(1)}, u32[]{:S(2)}, u32[]{:S(2)}) collective-permute-start(bf16[144,1536]{1,0:T(8,128)(2,1)S(1)} %shard_map.64._after.q_ref), channel_id=1, source_target_pairs={{0,4},{4,0},{8,12},{12,8},{16,20},{20,16},{24,28},{28,24},{32,36},... | collective-permute-start | bytes 1327112 | tf_op jit(solution)/shard_map/ppermute | solution.py:317
  5.6 19.3 %collective-permute-start.4 = (bf16[144,1536]{1,0:T(8,128)(2,1)S(1)}, bf16[144,1536]{1,0:T(8,128)(2,1)S(1)}, u32[]{:S(2)}, u32[]{:S(2)}) collective-permute-start(bf16[144,1536]{1,0:T(8,128)(2,1)S(1)} %shard_map.64._after.q_ref), channel_id=1, source_target_pairs={{0,252},{4,8},{8,4},{12,16},{16,12},{20,24},{24,20},{28,32},{32,28... | collective-permute-start | bytes 1327112 | tf_op jit(solution)/shard_map/ppermute | solution.py:317
  15.1 7.3 %collective-permute-start = (s32[8]{0:T(128)S(1)}, s32[8]{0:T(128)S(1)}, u32[]{:S(2)}, u32[]{:S(2)}) collective-permute-start(s32[8]{0:T(128)S(1)} %compare_select_fusion.ids_ref), channel_id=1, source_target_pairs={{0,8},{4,12},{8,0},{12,4},{16,24},{20,28},{24,16},{28,20},{32,40},... | collective-permute-start | bytes 104 | tf_op jit(solution)/shard_map/ppermute | solution.py:317
  15.1 9.8 %collective-permute-start.7 = (s32[8]{0:T(128)S(1)}, s32[8]{0:T(128)S(1)}, u32[]{:S(2)}, u32[]{:S(2)}) collective-permute-start(s32[8]{0:T(128)S(1)} %compare_select_fusion.ids_ref), channel_id=1, source_target_pairs={{0,248},{4,252},{8,16},{12,20},{16,8},{20,12},{24,32},{28,36},{32,... | collective-permute-start | bytes 104 | tf_op jit(solution)/shard_map/ppermute | solution.py:317
  16.8 1.0 %copy-start.2 = (bf16[4,16,2,1536]{3,2,1,0:T(2,128)(2,1)S(1)}, bf16[4,16,2,1536]{3,2,1,0:T(2,128)(2,1)}, u32[]{:S(2)}) copy-start(bf16[4,16,2,1536]{3,2,1,0:T(2,128)(2,1)} %k_ref.3) | copy-start | bytes 1179652
  17.8 1.0 %copy-start.3 = (bf16[4,16,2,1536]{3,2,1,0:T(2,128)(2,1)S(1)}, bf16[4,16,2,1536]{3,2,1,0:T(2,128)(2,1)}, u32[]{:S(2)}) copy-start(bf16[4,16,2,1536]{3,2,1,0:T(2,128)(2,1)} %v_ref.3) | copy-start | bytes 1179652
  18.9 16.4 %collective-permute-start.2 = (bf16[256,1536]{1,0:T(8,128)(2,1)S(1)}, bf16[256,1536]{1,0:T(8,128)(2,1)S(1)}, u32[]{:S(2)}, u32[]{:S(2)}) collective-permute-start(bf16[256,1536]{1,0:T(8,128)(2,1)S(1)} %shard_map.65.own_ref), channel_id=1, source_target_pairs={{1,2},{2,1},{5,6},{6,5},{9,10},{10,9},{13,14},{14,13},{17,18},{18,... | collective-permute-start | bytes 2359304 | tf_op jit(solution)/shard_map/ppermute | solution.py:317
  22.6 12.7 %collective-permute-start.1 = (bf16[256,1536]{1,0:T(8,128)(2,1)S(1)}, bf16[256,1536]{1,0:T(8,128)(2,1)S(1)}, u32[]{:S(2)}, u32[]{:S(2)}) collective-permute-start(bf16[256,1536]{1,0:T(8,128)(2,1)S(1)} %shard_map.66), channel_id=1, source_target_pairs={{0,1},{1,0},{2,3},{3,2},{4,5},{5,4},{6,7},{7,6},{8,9},{9,8},{10,11... | collective-permute-start | bytes 2359304 | tf_op jit(solution)/shard_map/ppermute | solution.py:317
  22.9 12.3 %copy-start = (bf16[512,1536]{1,0:T(8,128)(2,1)}, bf16[512,1536]{1,0:T(8,128)(2,1)S(1)}, u32[]{:S(2)}) copy-start(bf16[512,1536]{1,0:T(8,128)(2,1)S(1)} %shard_map.67.bank_ref) | copy-start | bytes 4718596
  25.7 26.4 %collective-permute-start.8 = (bf16[256,1536]{1,0:T(8,128)(2,1)S(1)}, bf16[256,1536]{1,0:T(8,128)(2,1)S(1)}, u32[]{:S(2)}, u32[]{:S(2)}) collective-permute-start(bf16[256,1536]{1,0:T(8,128)(2,1)S(1)} %get-tuple-element.27), channel_id=1, source_target_pairs={{0,4},{4,0},{8,12},{12,8},{16,20},{20,16},{24,28},{28,24},{32,36},... | collective-permute-start | bytes 2359304 | tf_op jit(solution)/shard_map/ppermute | solution.py:317
  26.5 25.6 %collective-permute-start.9 = (bf16[256,1536]{1,0:T(8,128)(2,1)S(1)}, bf16[256,1536]{1,0:T(8,128)(2,1)S(1)}, u32[]{:S(2)}, u32[]{:S(2)}) collective-permute-start(bf16[256,1536]{1,0:T(8,128)(2,1)S(1)} %get-tuple-element.28), channel_id=1, source_target_pairs={{0,252},{4,8},{8,4},{12,16},{16,12},{20,24},{24,20},{28,32},{32,28... | collective-permute-start | bytes 2359304 | tf_op jit(solution)/shard_map/ppermute | solution.py:317
  40.0 18.9 %collective-permute-start.5 = (s16[128,1664]{1,0:T(8,128)(2,1)S(1)}, s16[128,1664]{1,0:T(8,128)(2,1)S(1)}, u32[]{:S(2)}, u32[]{:S(2)}) collective-permute-start(s16[128,1664]{1,0:T(8,128)(2,1)S(1)} %get-tuple-element.19._after), channel_id=1, source_target_pairs={{0,4},{4,0},{8,12},{12,8},{16,20},{20,16},{24,28},{28,24},{32,36},... | collective-permute-start | bytes 1277960 | tf_op jit(solution)/shard_map/ppermute | solution.py:317
  40.1 18.8 %collective-permute-start.6 = (s16[128,1664]{1,0:T(8,128)(2,1)S(1)}, s16[128,1664]{1,0:T(8,128)(2,1)S(1)}, u32[]{:S(2)}, u32[]{:S(2)}) collective-permute-start(s16[128,1664]{1,0:T(8,128)(2,1)S(1)} %get-tuple-element.22), channel_id=1, source_target_pairs={{0,252},{4,8},{8,4},{12,16},{16,12},{20,24},{24,20},{28,32},{32,28... | collective-permute-start | bytes 1277960 | tf_op jit(solution)/shard_map/ppermute | solution.py:317
  55.1 8.7 %collective-permute-start.10 = (s16[128,1664]{1,0:T(8,128)(2,1)S(1)}, s16[128,1664]{1,0:T(8,128)(2,1)S(1)}, u32[]{:S(2)}, u32[]{:S(2)}) collective-permute-start(s16[128,1664]{1,0:T(8,128)(2,1)S(1)} %get-tuple-element.29), channel_id=1, source_target_pairs={{0,4},{4,0},{8,12},{12,8},{16,20},{20,16},{24,28},{28,24},{32,36},... | collective-permute-start | bytes 1277960 | tf_op jit(solution)/shard_map/ppermute | solution.py:317
  55.2 14.4 %collective-permute-start.11 = (s16[128,1664]{1,0:T(8,128)(2,1)S(1)}, s16[128,1664]{1,0:T(8,128)(2,1)S(1)}, u32[]{:S(2)}, u32[]{:S(2)}) collective-permute-start(s16[128,1664]{1,0:T(8,128)(2,1)S(1)} %get-tuple-element.30), channel_id=1, source_target_pairs={{0,252},{4,8},{8,4},{12,16},{16,12},{20,24},{24,20},{28,32},{32,28... | collective-permute-start | bytes 1277960 | tf_op jit(solution)/shard_map/ppermute | solution.py:317

commit v4 on v3

--- a/solution.py
+++ b/solution.py
@@ -292,7 +292,7 @@
     return total
 
 
-def merge_near(own_ref, stat_ref, a_ref, b_ref, out_ref):
+def merge_near(own_ref, stat_ref, b_ref, a_ref, out_ref):
     shares = shares_of(stat_ref[:, :STAT], stat_ref[:, STAT:], (a_ref, b_ref))
     for head in range(own_ref.shape[1] // HEAD_DIM):
         out_ref[:, columns(head)] = mixed_by(shares, own_ref, (a_ref, b_ref), head)
@@ -375,7 +375,7 @@
         scratch=[pltpu.VMEM((2 * rows, width), jnp.float32)],
     )
     back_b_far, back_a_far = swapped(b_far, 1), swapped(a_far, 0)
-    near = call(merge_near, plain, [VMEM] * 4, near, own_stat, back_a_near, back_b_near)
+    near = call(merge_near, plain, [VMEM] * 4, near, own_stat, back_b_near, back_a_near)
     return call(
         merge_far, shape(queries.shape, jnp.bfloat16), [VMEM] * 5, near, far, own_stat, back_a_far, back_b_far
     )

time: 71.9 us -> 71.3 us (level)
  the two profiles are of different devices: /device:TPU:1 before, /device:TPU:2 now
where the time goes in v4:
time: 71.3 us; the launch traced here: 71.1 us
  starting transfers between devices  31.6 us (44%)
  Pallas kernels  21.3 us (30%)
  waiting for transfers between devices  13.7 us (19%)
  local copies, waits for them, and re-layouts  3 us (4%)
  between operations  0.83 us (1%)
    ppermute x12, starting transfers between devices, swapped(): return lax.ppermute(value, axis, pairs)  31.6 us
    pallas_call x11, Pallas kernels, call(): pl.pallas_call(body, out_shape=out_shape, in_specs=in_specs, out_specs=VM...  21.3 us
    ppermute x12, waiting for transfers between devices, swapped(): return lax.ppermute(value, axis, pairs)  13.7 us
    unnamed x10, local copies, waits for them, and re-layouts  3 us
  transfers between devices with their start and end apart: 12, of which 3 were waited for; matrix products, arithmetic and copies ran while one was open for 0% of the time, Pallas kernels for 27%

profile of v4, /device:TPU:2, one launch (start us, length us, event | category | flops | bytes accessed | tf_op | source)
XLA Modules:
  0.0 71.1 jit_solution(4370243545392655998)
XLA Ops:
  0.7 0.7 compare_select_fusion.ids_ref
  1.3 1.0 %copy-done.4 = bf16[4,16,2,1536]{3,2,1,0:T(2,128)(2,1)S(1)} copy-done((bf16[4,16,2,1536]{3,2,1,0:T(2,128)(2,1)S(1)}, bf16[4,16,2,1536]{3,2,1,0:T(2,128)(2,1)}, u32[]{:S(2)}) %copy-start.4) | copy-done | bytes 393240
  2.3 0.7 shard_map.64._after.q_ref
  3.0 2.0 %collective-permute-start.3 = (bf16[144,1536]{1,0:T(8,128)(2,1)S(1)}, bf16[144,1536]{1,0:T(8,128)(2,1)S(1)}, u32[]{:S(2)}, u32[]{:S(2)}) collective-permute-start(bf16[144,1536]{1,0:T(8,128)(2,1)S(1)} %shard_map.64._after.q_ref), channel_id=1, source_target_pairs={{0,4},{4,0},{8,12},{12,8},{16,20},{20,16},{24,28},{28,24},{32,36},... | collective-permute-start | bytes 1327112 | tf_op jit(solution)/shard_map/ppermute | solution.py:317
  5.0 9.0 %collective-permute-start.4 = (bf16[144,1536]{1,0:T(8,128)(2,1)S(1)}, bf16[144,1536]{1,0:T(8,128)(2,1)S(1)}, u32[]{:S(2)}, u32[]{:S(2)}) collective-permute-start(bf16[144,1536]{1,0:T(8,128)(2,1)S(1)} %shard_map.64._after.q_ref), channel_id=1, source_target_pairs={{0,252},{4,8},{8,4},{12,16},{16,12},{20,24},{24,20},{28,32},{32,28... | collective-permute-start | bytes 1327112 | tf_op jit(solution)/shard_map/ppermute | solution.py:317
  14.0 1.9 %collective-permute-start.7 = (s32[8]{0:T(128)S(1)}, s32[8]{0:T(128)S(1)}, u32[]{:S(2)}, u32[]{:S(2)}) collective-permute-start(s32[8]{0:T(128)S(1)} %compare_select_fusion.ids_ref), channel_id=1, source_target_pairs={{0,248},{4,252},{8,16},{12,20},{16,8},{20,12},{24,32},{28,36},{32,... | collective-permute-start | bytes 104 | tf_op jit(solution)/shard_map/ppermute | solution.py:317
  15.9 1.0 %copy-done.2 = bf16[4,16,2,1536]{3,2,1,0:T(2,128)(2,1)S(1)} copy-done((bf16[4,16,2,1536]{3,2,1,0:T(2,128)(2,1)S(1)}, bf16[4,16,2,1536]{3,2,1,0:T(2,128)(2,1)}, u32[]{:S(2)}) %copy-start.2) | copy-done | bytes 393240
  16.9 1.0 %copy-done.3 = bf16[4,16,2,1536]{3,2,1,0:T(2,128)(2,1)S(1)} copy-done((bf16[4,16,2,1536]{3,2,1,0:T(2,128)(2,1)S(1)}, bf16[4,16,2,1536]{3,2,1,0:T(2,128)(2,1)}, u32[]{:S(2)}) %copy-start.3) | copy-done | bytes 393240
  18.0 1.9 %collective-permute-start.2 = (bf16[256,1536]{1,0:T(8,128)(2,1)S(1)}, bf16[256,1536]{1,0:T(8,128)(2,1)S(1)}, u32[]{:S(2)}, u32[]{:S(2)}) collective-permute-start(bf16[256,1536]{1,0:T(8,128)(2,1)S(1)} %shard_map.65.own_ref), channel_id=1, source_target_pairs={{1,2},{2,1},{5,6},{6,5},{9,10},{10,9},{13,14},{14,13},{17,18},{18,... | collective-permute-start | bytes 2359304 | tf_op jit(solution)/shard_map/ppermute | solution.py:317
  20.1 0.2 shard_map.67.bank_ref
  20.3 4.0 %collective-permute-done.7.second_ref = s32[8]{0:T(128)S(1)} collective-permute-done((s32[8]{0:T(128)S(1)}, s32[8]{0:T(128)S(1)}, u32[]{:S(2)}, u32[]{:S(2)}) %collective-permute-start.7) | collective-permute-done | bytes 64 | tf_op jit(solution)/shard_map/ppermute | solution.py:317
  24.3 0.8 %shard_map.72 = (bf16[256,1536]{1,0:T(8,128)(2,1)S(1)}, bf16[256,1536]{1,0:T(8,128)(2,1)S(1)}) custom-call(bf16[512,1536]{1,0:T(8,128)(2,1)S(1)} %shard_map.67.bank_ref, s32[8]{0:T(128)S(1)} %collective-permute-done._after.first_ref, s32[8]{0:T(128)S(1)} %collective-permute-done.7.second_ref, bf16[144,1536]{1,0:T(8,128)(2,1)S(1)} %collective-permute-done.3.a_ref._one, ...), custom_call_target="tpu_custom_call" | custom-call | tf_op jit(solution)/shard_map/pallas_call | solution.py:31
  25.1 1.1 %collective-permute-start.8 = (bf16[256,1536]{1,0:T(8,128)(2,1)S(1)}, bf16[256,1536]{1,0:T(8,128)(2,1)S(1)}, u32[]{:S(2)}, u32[]{:S(2)}) collective-permute-start(bf16[256,1536]{1,0:T(8,128)(2,1)S(1)} %get-tuple-element.27), channel_id=1, source_target_pairs={{0,4},{4,0},{8,12},{12,8},{16,20},{20,16},{24,28},{28,24},{32,36},... | collective-permute-start | bytes 2359304 | tf_op jit(solution)/shard_map/ppermute | solution.py:317
  26.2 7.5 %collective-permute-start.9 = (bf16[256,1536]{1,0:T(8,128)(2,1)S(1)}, bf16[256,1536]{1,0:T(8,128)(2,1)S(1)}, u32[]{:S(2)}, u32[]{:S(2)}) collective-permute-start(bf16[256,1536]{1,0:T(8,128)(2,1)S(1)} %get-tuple-element.28), channel_id=1, source_target_pairs={{0,252},{4,8},{8,4},{12,16},{16,12},{20,24},{24,20},{28,32},{32,28... | collective-permute-start | bytes 2359304 | tf_op jit(solution)/shard_map/ppermute | solution.py:317
  33.7 1.8 %shard_map.68 = (f32[128,1536]{1,0:T(8,128)S(1)}, f32[128,1536]{1,0:T(8,128)S(1)}, f32[128,384]{1,0:T(8,128)S(1)}, f32[128,384]{1,0:T(8,128)S(1)}) custom-call(bf16[144,1536]{1,0:T(8,128)(2,1)S(1)} %collective-permute-done.3.a_ref._one, bf16[144,1536]{1,0:T(8,128)(2,1)S(1)} %collective-permute-done.4.b_ref._two, bf16[512,1536]{1,0:T(8,128)(2,1)S(1)} %shard_map.67.bank_ref, ...), custom_call_target="tpu_custom_call" | custom-call | tf_op jit(solution)/shard_map/pallas_call | solution.py:31
  35.6 4.8 %shard_map.69 = (s16[128,1664]{1,0:T(8,128)(2,1)S(1)}, s16[128,1664]{1,0:T(8,128)(2,1)S(1)}) custom-call(bf16[144,1536]{1,0:T(8,128)(2,1)S(1)} %collective-permute-done.3.a_ref._one, bf16[144,1536]{1,0:T(8,128)(2,1)S(1)} %collective-permute-done.4.b_ref._two, bf16[256,1536]{1,0:T(8,128)(2,1)S(1)} %shard_map.65.own_ref, ...), custom_call_target="tpu_custom_call" | custom-call | tf_op jit(solution)/shard_map/pallas_call | solution.py:31
  40.3 0.3 collective-permute-start.5
  40.7 7.5 %shard_map.70 = (f32[128,1536]{1,0:T(8,128)S(1)}, f32[128,1536]{1,0:T(8,128)S(1)}, f32[128,256]{1,0:T(8,128)S(1)}) custom-call(bf16[144,1536]{1,0:T(8,128)(2,1)S(1)} %shard_map.64._after.q_ref, bf16[256,1536]{1,0:T(8,128)(2,1)S(1)} %shard_map.65.own_ref, bf16[256,1536]{1,0:T(8,128)(2,1)S(1)} %collective-permute-done.1.mate_ref, ...), custom_call_target="tpu_custom_call" | custom-call | tf_op jit(solution)/shard_map/pallas_call | solution.py:31
  48.2 4.2 %collective-permute-done.9.b_pack = bf16[256,1536]{1,0:T(8,128)(2,1)S(1)} collective-permute-done((bf16[256,1536]{1,0:T(8,128)(2,1)S(1)}, bf16[256,1536]{1,0:T(8,128)(2,1)S(1)}, u32[]{:S(2)}, u32[]{:S(2)}) %collective-permute-start.9) | collective-permute-done | bytes 786464 | tf_op jit(solution)/shard_map/ppermute | solution.py:317
  52.4 2.9 %shard_map.73 = (s16[128,1664]{1,0:T(8,128)(2,1)S(1)}, s16[128,1664]{1,0:T(8,128)(2,1)S(1)}) custom-call(bf16[144,1536]{1,0:T(8,128)(2,1)S(1)} %collective-permute-done.3.a_ref._one, bf16[144,1536]{1,0:T(8,128)(2,1)S(1)} %collective-permute-done.4.b_ref._two, f32[128,1536]{1,0:T(8,128)S(1)} %get-tuple-element.24.a_part, ...), custom_call_target="tpu_custom_call" | custom-call | tf_op jit(solution)/shard_map/pallas_call | solution.py:31
  55.5 7.6 %collective-permute-start.11 = (s16[128,1664]{1,0:T(8,128)(2,1)S(1)}, s16[128,1664]{1,0:T(8,128)(2,1)S(1)}, u32[]{:S(2)}, u32[]{:S(2)}) collective-permute-start(s16[128,1664]{1,0:T(8,128)(2,1)S(1)} %get-tuple-element.30), channel_id=1, source_target_pairs={{0,252},{4,8},{8,4},{12,16},{16,12},{20,24},{24,20},{28,32},{32,28... | collective-permute-start | bytes 1277960 | tf_op jit(solution)/shard_map/ppermute | solution.py:317
  63.1 0.8 %shard_map.71.near_ref = f32[128,1536]{1,0:T(8,128)S(1)} custom-call(f32[128,1536]{1,0:T(8,128)S(1)} %get-tuple-element.20.own_ref, f32[128,256]{1,0:T(8,128)S(1)} %get-tuple-element.21.stat_ref._after, s16[128,1664]{1,0:T(8,128)(2,1)S(1)} %collective-permute-done.5.b_ref, s16[128,1664]{1,0:T(8,128)(2,1)S(1)} %collective-permute-done.6.a_ref), custom_call_target="tpu_custom_call" | custom-call | tf_op jit(solution)/shard_map/pallas_call | solution.py:31
  63.9 5.5 %collective-permute-done.11.b_ref = s16[128,1664]{1,0:T(8,128)(2,1)S(1)} collective-permute-done((s16[128,1664]{1,0:T(8,128)(2,1)S(1)}, s16[128,1664]{1,0:T(8,128)(2,1)S(1)}, u32[]{:S(2)}, u32[]{:S(2)}) %collective-permute-start.11) | collective-permute-done | bytes 426016 | tf_op jit(solution)/shard_map/ppermute | solution.py:317
  69.4 1.7 %shard_map.74 = bf16[4,16,2,1536]{3,2,1,0:T(2,128)(2,1)} custom-call(f32[128,1536]{1,0:T(8,128)S(1)} %shard_map.71.near_ref, f32[128,1536]{1,0:T(8,128)S(1)} %get-tuple-element.23.own_ref, f32[128,256]{1,0:T(8,128)S(1)} %get-tuple-element.21.stat_ref._after, s16[128,1664]{1,0:T(8,128)(2,1)S(1)} %collective-permute-done.10.a_ref, ...), custom_call_target="tpu_custom_call" | custom-call | tf_op jit(solution)/shard_map/pallas_call | solution.py:31
  (22 shorter events, 0.5 us)
Async XLA Ops:
  1.3 1.0 %copy-start.4 = (bf16[4,16,2,1536]{3,2,1,0:T(2,128)(2,1)S(1)}, bf16[4,16,2,1536]{3,2,1,0:T(2,128)(2,1)}, u32[]{:S(2)}) copy-start(bf16[4,16,2,1536]{3,2,1,0:T(2,128)(2,1)} %q_ref.1) | copy-start | bytes 1179652
  3.0 17.1 %copy-start.1 = (bf16[2,8,16,2,1536]{4,3,2,1,0:T(2,128)(2,1)S(1)}, bf16[2,8,16,2,1536]{4,3,2,1,0:T(2,128)(2,1)}, u32[]{:S(2)}) copy-start(bf16[2,8,16,2,1536]{4,3,2,1,0:T(2,128)(2,1)} %bank_ref.1) | copy-start | bytes 4718596
  3.0 21.3 %collective-permute-start.3 = (bf16[144,1536]{1,0:T(8,128)(2,1)S(1)}, bf16[144,1536]{1,0:T(8,128)(2,1)S(1)}, u32[]{:S(2)}, u32[]{:S(2)}) collective-permute-start(bf16[144,1536]{1,0:T(8,128)(2,1)S(1)} %shard_map.64._after.q_ref), channel_id=1, source_target_pairs={{0,4},{4,0},{8,12},{12,8},{16,20},{20,16},{24,28},{28,24},{32,36},... | collective-permute-start | bytes 1327112 | tf_op jit(solution)/shard_map/ppermute | solution.py:317
  5.0 19.3 %collective-permute-start.4 = (bf16[144,1536]{1,0:T(8,128)(2,1)S(1)}, bf16[144,1536]{1,0:T(8,128)(2,1)S(1)}, u32[]{:S(2)}, u32[]{:S(2)}) collective-permute-start(bf16[144,1536]{1,0:T(8,128)(2,1)S(1)} %shard_map.64._after.q_ref), channel_id=1, source_target_pairs={{0,252},{4,8},{8,4},{12,16},{16,12},{20,24},{24,20},{28,32},{32,28... | collective-permute-start | bytes 1327112 | tf_op jit(solution)/shard_map/ppermute | solution.py:317
  14.0 5.9 %collective-permute-start = (s32[8]{0:T(128)S(1)}, s32[8]{0:T(128)S(1)}, u32[]{:S(2)}, u32[]{:S(2)}) collective-permute-start(s32[8]{0:T(128)S(1)} %compare_select_fusion.ids_ref), channel_id=1, source_target_pairs={{0,8},{4,12},{8,0},{12,4},{16,24},{20,28},{24,16},{28,20},{32,40},... | collective-permute-start | bytes 104 | tf_op jit(solution)/shard_map/ppermute | solution.py:317
  14.0 10.3 %collective-permute-start.7 = (s32[8]{0:T(128)S(1)}, s32[8]{0:T(128)S(1)}, u32[]{:S(2)}, u32[]{:S(2)}) collective-permute-start(s32[8]{0:T(128)S(1)} %compare_select_fusion.ids_ref), channel_id=1, source_target_pairs={{0,248},{4,252},{8,16},{12,20},{16,8},{20,12},{24,32},{28,36},{32,... | collective-permute-start | bytes 104 | tf_op jit(solution)/shard_map/ppermute | solution.py:317
  15.9 1.0 %copy-start.2 = (bf16[4,16,2,1536]{3,2,1,0:T(2,128)(2,1)S(1)}, bf16[4,16,2,1536]{3,2,1,0:T(2,128)(2,1)}, u32[]{:S(2)}) copy-start(bf16[4,16,2,1536]{3,2,1,0:T(2,128)(2,1)} %k_ref.3) | copy-start | bytes 1179652
  16.9 1.0 %copy-start.3 = (bf16[4,16,2,1536]{3,2,1,0:T(2,128)(2,1)S(1)}, bf16[4,16,2,1536]{3,2,1,0:T(2,128)(2,1)}, u32[]{:S(2)}) copy-start(bf16[4,16,2,1536]{3,2,1,0:T(2,128)(2,1)} %v_ref.3) | copy-start | bytes 1179652
  18.0 17.6 %collective-permute-start.2 = (bf16[256,1536]{1,0:T(8,128)(2,1)S(1)}, bf16[256,1536]{1,0:T(8,128)(2,1)S(1)}, u32[]{:S(2)}, u32[]{:S(2)}) collective-permute-start(bf16[256,1536]{1,0:T(8,128)(2,1)S(1)} %shard_map.65.own_ref), channel_id=1, source_target_pairs={{1,2},{2,1},{5,6},{6,5},{9,10},{10,9},{13,14},{14,13},{17,18},{18,... | collective-permute-start | bytes 2359304 | tf_op jit(solution)/shard_map/ppermute | solution.py:317
  20.0 15.5 %collective-permute-start.1 = (bf16[256,1536]{1,0:T(8,128)(2,1)S(1)}, bf16[256,1536]{1,0:T(8,128)(2,1)S(1)}, u32[]{:S(2)}, u32[]{:S(2)}) collective-permute-start(bf16[256,1536]{1,0:T(8,128)(2,1)S(1)} %shard_map.66), channel_id=1, source_target_pairs={{0,1},{1,0},{2,3},{3,2},{4,5},{5,4},{6,7},{7,6},{8,9},{9,8},{10,11... | collective-permute-start | bytes 2359304 | tf_op jit(solution)/shard_map/ppermute | solution.py:317
  20.3 15.2 %copy-start = (bf16[512,1536]{1,0:T(8,128)(2,1)}, bf16[512,1536]{1,0:T(8,128)(2,1)S(1)}, u32[]{:S(2)}) copy-start(bf16[512,1536]{1,0:T(8,128)(2,1)S(1)} %shard_map.67.bank_ref) | copy-start | bytes 4718596
  25.1 23.1 %collective-permute-start.8 = (bf16[256,1536]{1,0:T(8,128)(2,1)S(1)}, bf16[256,1536]{1,0:T(8,128)(2,1)S(1)}, u32[]{:S(2)}, u32[]{:S(2)}) collective-permute-start(bf16[256,1536]{1,0:T(8,128)(2,1)S(1)} %get-tuple-element.27), channel_id=1, source_target_pairs={{0,4},{4,0},{8,12},{12,8},{16,20},{20,16},{24,28},{28,24},{32,36},... | collective-permute-start | bytes 2359304 | tf_op jit(solution)/shard_map/ppermute | solution.py:317
  26.2 26.2 %collective-permute-start.9 = (bf16[256,1536]{1,0:T(8,128)(2,1)S(1)}, bf16[256,1536]{1,0:T(8,128)(2,1)S(1)}, u32[]{:S(2)}, u32[]{:S(2)}) collective-permute-start(bf16[256,1536]{1,0:T(8,128)(2,1)S(1)} %get-tuple-element.28), channel_id=1, source_target_pairs={{0,252},{4,8},{8,4},{12,16},{16,12},{20,24},{24,20},{28,32},{32,28... | collective-permute-start | bytes 2359304 | tf_op jit(solution)/shard_map/ppermute | solution.py:317
  40.3 22.7 %collective-permute-start.5 = (s16[128,1664]{1,0:T(8,128)(2,1)S(1)}, s16[128,1664]{1,0:T(8,128)(2,1)S(1)}, u32[]{:S(2)}, u32[]{:S(2)}) collective-permute-start(s16[128,1664]{1,0:T(8,128)(2,1)S(1)} %get-tuple-element.22), channel_id=1, source_target_pairs={{0,252},{4,8},{8,4},{12,16},{16,12},{20,24},{24,20},{28,32},{32,28... | collective-permute-start | bytes 1277960 | tf_op jit(solution)/shard_map/ppermute | solution.py:317
  40.6 22.4 %collective-permute-start.6 = (s16[128,1664]{1,0:T(8,128)(2,1)S(1)}, s16[128,1664]{1,0:T(8,128)(2,1)S(1)}, u32[]{:S(2)}, u32[]{:S(2)}) collective-permute-start(s16[128,1664]{1,0:T(8,128)(2,1)S(1)} %get-tuple-element.19._after), channel_id=1, source_target_pairs={{0,4},{4,0},{8,12},{12,8},{16,20},{20,16},{24,28},{28,24},{32,36},... | collective-permute-start | bytes 1277960 | tf_op jit(solution)/shard_map/ppermute | solution.py:317
  55.4 8.5 %collective-permute-start.10 = (s16[128,1664]{1,0:T(8,128)(2,1)S(1)}, s16[128,1664]{1,0:T(8,128)(2,1)S(1)}, u32[]{:S(2)}, u32[]{:S(2)}) collective-permute-start(s16[128,1664]{1,0:T(8,128)(2,1)S(1)} %get-tuple-element.29), channel_id=1, source_target_pairs={{0,4},{4,0},{8,12},{12,8},{16,20},{20,16},{24,28},{28,24},{32,36},... | collective-permute-start | bytes 1277960 | tf_op jit(solution)/shard_map/ppermute | solution.py:317
  55.5 13.9 %collective-permute-start.11 = (s16[128,1664]{1,0:T(8,128)(2,1)S(1)}, s16[128,1664]{1,0:T(8,128)(2,1)S(1)}, u32[]{:S(2)}, u32[]{:S(2)}) collective-permute-start(s16[128,1664]{1,0:T(8,128)(2,1)S(1)} %get-tuple-element.30), channel_id=1, source_target_pairs={{0,252},{4,8},{8,4},{12,16},{16,12},{20,24},{24,20},{28,32},{32,28... | collective-permute-start | bytes 1277960 | tf_op jit(solution)/shard_map/ppermute | solution.py:317
